TPU v7x, 32 devices: a whole 2x2x4 slice. The times are simulated.
32 devices in a mesh: line: 4 (over y, x), surf: 8 (over z, core).
Axes of the slice: x: 2, y: 2, z: 4, core: 2. Of those that a mesh axis runs over, the one named last changes fastest.
Arguments:
- face_coef: float32 [16, 1024], P('line', 'surf'), may hold values from 0.5 to 2
- face_mix: float32 [16, 17, 17, 1024], P('line', None, None, 'surf'), may hold values from -0.6 to 0.6
- cell_mix: float32 [16, 17, 17, 1024], P('line', None, None, 'surf'), may hold values from -0.6 to 0.6
- time_term: float32 [16, 17, 1024], P('line', None, 'surf'), may hold values from 0.0005 to 1
- couple: float32 [16, 4, 17, 1024], P('line', None, None, 'surf'), may hold values from 0.0005 to 0.05
- rhs: float32 [16, 17, 1024], P('line', None, 'surf'), may hold values from -0.4 to 0.4
- start_delta: float32 [16, 17, 1024], P('line', None, 'surf'), may hold values from -6 to 6
- neighbours: int32 [4, 1024], P(None, 'surf'), may hold values from -1 to 1023, as said below
- wall_type: int32 [1024], P('surf'), may hold values from 0 to 2
Outputs:
- delta: float32 [16, 17, 1024], P('line', None, 'surf')
Inputs may be any that keep to these rules, and one draw needn't show every extreme that they name: `neighbours`: -1 marks a missing neighbour. Entries 0 and 1 of a line are -1 or lines of its own grid block (blocks are the aligned runs of 128 lines). Entry 2 is a line of its own block or one of the last 16 lines of the block before it; entry 3 a line of its own block or one of the first 16 lines of the block after it; blocks follow one another cyclically. A line is the neighbour of its neighbour. `wall_type`: 0 slip wall, 1 isothermal wall, 2 catalytic wall.
All inputs are finite; a program needn't handle non-finite values.
Results may differ from a plain program's by a relative error of at most 0.0003.
Values sent between devices are 32-bit elements; how exact they have to be, the bound alone decides.
A program may use at most 64 MiB of HBM per device.

v0:
```python
import jax
import jax.numpy as jnp
from jax import lax
from jax.sharding import PartitionSpec as P

COLS = 16
ITERS = 2


wall_levels = (0.5, 4.0, 32.0)


def from_behind(value, axis, steps):
    count = lax.axis_size(axis)
    initial, last = (max(0, -steps), min(count, count - steps))
    return lax.ppermute(value, axis, [(source, source + steps) for source in range(initial, last)])


def padded_2(block, sides, width):
    for axis, dim in sides:
        count = lax.axis_size(axis)
        forward = [(i, i + 1) for i in range(count - 1)]
        forward.append((count - 1, 0))
        backward = [(target, source) for source, target in forward]
        low = lax.ppermute(
            lax.slice_in_dim(block, block.shape[dim] - width, None, axis=dim), axis, forward
        )
        high = lax.ppermute(lax.slice_in_dim(block, 0, width, axis=dim), axis, backward)
        block = jnp.concatenate([low, block, high], axis=dim)
    return block


def matrix_product(matrix_left, matrix_right):
    return jnp.sum(matrix_left[:, :, None, :] * matrix_right[None, :, :, :], axis=1)


def matrix_vector(matrix_left, vector_right):
    return jnp.sum(matrix_left * vector_right[None, :, :], axis=1)


def invert(matrix):
    width = matrix.shape[0]
    row_ids = jnp.arange(width)[:, None, None]
    working = matrix
    result = jnp.broadcast_to(jnp.eye(width, dtype=jnp.float32)[:, :, None], matrix.shape)
    for pivot_row in range(width):
        pivot = working[pivot_row, pivot_row]
        row_work = working[pivot_row] / pivot
        row_result = result[pivot_row] / pivot
        factors = working[:, pivot_row]
        is_pivot = row_ids == pivot_row
        working = jnp.where(
            is_pivot, row_work[None], working - factors[:, None, :] * row_work[None]
        )
        result = jnp.where(
            is_pivot, row_result[None], result - factors[:, None, :] * row_result[None]
        )
    return result


def on_device(
    face_coef, face_mix, cell_mix, time_term, couple, rhs, start_delta, neighbours, wall_type
):
    cells, width, _, lines = face_mix.shape
    inner_cells = cells - 1
    identity = jnp.eye(width, dtype=jnp.float32)[:, :, None]
    line_place = lax.axis_index("line")
    is_first = (line_place == 0).astype(jnp.float32)
    wall_term = jnp.zeros(wall_type.shape, jnp.float32)
    for wall_kind, wall_value in enumerate(wall_levels):
        wall_term = wall_term + jnp.where(wall_type == wall_kind, wall_value, 0.0).astype(
            jnp.float32
        )
    below_coef, below_mix = from_behind((face_coef[-1], face_mix[-1]), "line", 1)
    coef_below = jnp.concatenate([below_coef[None], face_coef[:-1]], 0)
    mix_below = jnp.concatenate([below_mix[None], face_mix[:-1]], 0)
    coef_diag = (coef_below + face_coef).at[0].add(is_first * wall_term)
    diag_extra = time_term + jnp.sum(couple, axis=1)
    diagonal = (
        identity[None] * diag_extra[:, None]
        + coef_diag[:, None, None] * identity[None]
        + cell_mix
        - jnp.swapaxes(cell_mix, 1, 2)
    )
    lower = -coef_below[:, None, None] * identity[None] - jnp.swapaxes(mix_below, 1, 2)
    upper = -face_coef[:, None, None] * identity[None] + face_mix
    lower_inner = lower[:inner_cells].at[0].set(0.0)
    source_left = jnp.zeros_like(lower_inner).at[0].set(lower[0])
    zero_matrix = jnp.zeros((width, width, lines), jnp.float32)
    zero_vector = jnp.zeros((width, lines), jnp.float32)

    def factor_step(state_prev, inputs):
        coupler_prev, left_prev = state_prev
        block_diag, block_lower, block_upper, block_source = inputs
        inverse = invert(block_diag - matrix_product(block_lower, coupler_prev))
        coupler_now = matrix_product(inverse, block_upper)
        left_now = matrix_product(inverse, block_source - matrix_product(block_lower, left_prev))
        return ((coupler_now, left_now), (inverse, coupler_now, left_now))

    _, (inverses, couplers, forward_left) = lax.scan(
        factor_step,
        (zero_matrix, zero_matrix),
        (diagonal[:inner_cells], lower_inner, upper[:inner_cells], source_left),
    )

    def back_matrix(state_above, inputs):
        left_above, right_above = state_above
        coupler, left_forward = inputs
        left_now = left_forward - matrix_product(coupler, left_above)
        right_now = -matrix_product(coupler, right_above)
        return ((left_now, right_now), (left_now, right_now))

    minus_identity = -jnp.broadcast_to(identity, (width, width, lines))
    _, (left_part, right_part) = lax.scan(
        back_matrix, (zero_matrix, minus_identity), (couplers, forward_left), reverse=True
    )
    left_next, right_next = from_behind((left_part[0], right_part[0]), "line", -1)
    last_lower = lower[-1]
    last_upper = upper[-1]
    red_lower = -matrix_product(last_lower, left_part[-1])
    red_diag = (
        diagonal[-1]
        - matrix_product(last_lower, right_part[-1])
        - matrix_product(last_upper, left_next)
    )
    red_upper = -matrix_product(last_upper, right_next)
    all_lower, all_diag, all_upper = (
        lax.all_gather(red_lower[None], "line", axis=0, tiled=True),
        lax.all_gather(red_diag[None], "line", axis=0, tiled=True),
        lax.all_gather(red_upper[None], "line", axis=0, tiled=True),
    )

    def chain_factor(coupler_prev, inputs):
        block_lower, block_diag, block_upper = inputs
        inverse = invert(block_diag - matrix_product(block_lower, coupler_prev))
        coupler_now = matrix_product(inverse, block_upper)
        return (coupler_now, (inverse, coupler_now))

    _, (chain_inverse, chain_coupler) = lax.scan(
        chain_factor, zero_matrix, (all_lower, all_diag, all_upper)
    )
    surf_place = lax.axis_index("surf")
    line_total = lines * lax.axis_size("surf")
    line_base = surf_place * lines - COLS
    valid = neighbours >= 0
    local_index = jnp.where(valid, (neighbours - line_base) % line_total, 0)
    weights = couple * valid.astype(jnp.float32)[None, :, None, :]

    def vector_forward(solved_prev, inputs):
        inverse, block_lower, source = inputs
        solved_now = matrix_vector(inverse, source - matrix_vector(block_lower, solved_prev))
        return (solved_now, solved_now)

    def vector_back(solved_above, inputs):
        coupler, forward_value = inputs
        solved_now = forward_value - matrix_vector(coupler, solved_above)
        return (solved_now, solved_now)

    previous = start_delta
    for sweep_number in range(ITERS):
        padded = padded_2(previous, (("surf", 2),), COLS)
        neighbour_vals = jnp.take(padded, local_index, axis=2)
        right_side = rhs + jnp.sum(weights * jnp.swapaxes(neighbour_vals, 1, 2), axis=1)
        _, forward_values = lax.scan(
            vector_forward, zero_vector, (inverses, lower_inner, right_side[:inner_cells])
        )
        _, particular = lax.scan(vector_back, zero_vector, (couplers, forward_values), reverse=True)
        start_next = from_behind(particular[0], "line", -1)
        red_right = (
            right_side[-1]
            - matrix_vector(last_lower, particular[-1])
            - matrix_vector(last_upper, start_next)
        )
        all_right = lax.all_gather(red_right[None], "line", axis=0, tiled=True)
        _, chain_forward = lax.scan(
            vector_forward, zero_vector, (chain_inverse, all_lower, all_right)
        )
        _, separators = lax.scan(
            vector_back, zero_vector, (chain_coupler, chain_forward), reverse=True
        )
        own_sep = lax.dynamic_index_in_dim(separators, line_place, 0, keepdims=False)
        below_place = jnp.maximum(line_place - 1, 0)
        left_sep = lax.dynamic_index_in_dim(separators, below_place, 0, keepdims=False) * (
            1.0 - is_first
        )
        interior = particular - jnp.sum(left_part * left_sep[None, None, :, :], axis=2)
        interior = interior - jnp.sum(right_part * own_sep[None, None, :, :], axis=2)
        previous = jnp.concatenate([interior, own_sep[None]], 0)
    return previous


def solution(mesh):
    placed = (
        P("line", "surf"),
        P("line", None, None, "surf"),
        P("line", None, None, "surf"),
        P("line", None, "surf"),
        P("line", None, None, "surf"),
        P("line", None, "surf"),
        P("line", None, "surf"),
        P(None, "surf"),
        P("surf"),
    )
    return jax.shard_map(
        on_device, mesh=mesh, in_specs=placed, out_specs=P("line", None, "surf"), check_vma=False
    )
```

profile of v0, /device:TPU:0, one launch (start us, length us, event | category | flops | bytes accessed | tf_op | source)
XLA Modules:
  0.0 221.1 jit_solution(10247728219049279712)
XLA Ops:
  0.8 4.8 %collective-permute-start = (f32[128]{0:T(128)S(1)}, f32[128]{0:T(128)S(1)}, u32[]{:S(2)}, u32[]{:S(2)}) collective-permute-start(f32[128]{0:T(128)S(1)} %slice_bitcast_fusion.44), channel_id=1, source_target_pairs={{0,8},{8,16},{16,24},{1,9},{9,17},{17,25},{2,10},{10,18},{18,26},{... | collective-permute-start | bytes 1544 | tf_op jit(solution)/shard_map/ppermute | solution.py:16
  6.9 3.4 %collective-permute-start.1 = (f32[17,17,128]{2,0,1:T(8,128)S(1)}, f32[17,17,128]{2,0,1:T(8,128)S(1)}, u32[]{:S(2)}, u32[]{:S(2)}) collective-permute-start(f32[17,17,128]{2,0,1:T(8,128)S(1)} %bitcast.930), channel_id=1, source_target_pairs={{0,8},{8,16},{16,24},{1,9},{9,17},{17,25},{2,10},{10,18},{18,26},{... | collective-permute-start | bytes 443912 | tf_op jit(solution)/shard_map/ppermute | solution.py:16
  11.3 3.5 %collective-permute-start.3 = (f32[4,17,16]{2,0,1:T(4,128)S(1)}, f32[4,17,16]{2,0,1:T(4,128)S(1)}, u32[]{:S(2)}, u32[]{:S(2)}) collective-permute-start(f32[4,17,16]{2,0,1:T(4,128)S(1)} %get-tuple-element.1259), channel_id=1, source_target_pairs={{1,0},{2,1},{3,2},{4,3},{5,4},{6,5},{7,6},{0,7},{9,8},{10,9},{11,1... | collective-permute-start | bytes 13064 | tf_op jit(solution)/shard_map/ppermute | solution.py:28
  18.0 2.1 gather_fusion
  20.7 1.8 copy_add_fusion
  27.0 28.3 %while.172 = (s32[]{:T(128)}, f32[17,17,128]{2,1,0:T(8,128)S(1)}, f32[17,17,128]{2,1,0:T(8,128)S(1)}, f32[3,17,17,128]{3,2,1,0:T(8,128)S(1)}, f32[3,17,17,128]{3...) while((s32[]{:T(128)}, f32[17,17,128]{2,1,0:T(8,128)S(1)}, ...), condition=%wide.region_6.7_spmd, body=%wide.region_1.6_spmd.sunk | while | flops 13019928 | bytes 15185637 | solution.py:100
  60.7 8.0 %while.179 = (s32[]{:T(128)}, f32[17,17,128]{2,1,0:T(8,128)}, f32[17,17,128]{2,1,0:T(8,128)S(1)}, f32[3,17,17,128]{3,2,1,0:T(8,128)S(1)}, f32[3,17,17,128]{3,2,1...) while((s32[]{:T(128)}, f32[17,17,128]{2,1,0:T(8,128)}, ...), condition=%wide.region_18.20_spmd.clone, body=%wide.region_15.19_spmd.clone.sunk | while | flops 2589444 | bytes 3029127 | solution.py:114
  73.1 20.1 %all-gather = f32[68,17,128]{2,1,0:T(8,128)S(1)} all-gather(f32[17,17,128]{2,1,0:T(8,128)S(1)} %neg.70), channel_id=2, replica_groups=mesh['line'=4,'surf'=8] {'line'}, dimensions={0}, use_global_device_ids=true | all-gather | bytes 739840 | tf_op jit(solution)/shard_map/all_gather | solution.py:128
  95.0 8.1 %all_gather.18 = f32[4,17,128]{2,1,0:T(8,128)} all-gather(f32[1,17,128]{2,1,0:T(8,128)S(1)} %copy.90), channel_id=1, replica_groups=mesh['line'=4,'surf'=8] {'line'}, dimensions={0}, use_global_device_ids=true | all-gather | bytes 43520 | tf_op jit(solution)/shard_map/all_gather | solution.py:174
  104.7 13.5 %all_gather.15 = f32[4,17,17,128]{3,2,1,0:T(8,128)} all-gather(f32[1,17,17,128]{3,2,1,0:T(8,128)S(1)} %fusion.91), channel_id=1, replica_groups=mesh['line'=4,'surf'=8] {'line'}, dimensions={0}, use_global_device_ids=true | all-gather | bytes 739840 | tf_op jit(solution)/shard_map/all_gather | solution.py:129
  118.2 11.2 %all-gather.1 = f32[68,17,128]{2,1,0:T(8,128)} all-gather(f32[17,17,128]{2,1,0:T(8,128)S(1)} %neg.72), channel_id=3, replica_groups=mesh['line'=4,'surf'=8] {'line'}, dimensions={0}, use_global_device_ids=true | all-gather | bytes 739840 | tf_op jit(solution)/shard_map/all_gather | solution.py:130
  129.4 36.0 %while.174 = (s32[]{:T(128)}, f32[17,17,128]{2,1,0:T(8,128)S(1)}, f32[4,17,17,128]{3,2,1,0:T(8,128)}, f32[4,17,17,128]{3,2,1,0:T(8,128)}, f32[4,17,17,128]{3,2,1...) while((s32[]{:T(128)}, f32[17,17,128]{2,1,0:T(8,128)S(1)}, ...), condition=%wide.region_26.28_spmd, body=%wide.region_23.27_spmd.sunk | while | flops 10541464 | bytes 13530722 | solution.py:139
  145.8 1.6 select_dynamic-update-slice_fusion.5
  165.4 7.1 %while.175 = (s32[]{:T(128)}, f32[17,128]{1,0:T(8,128)S(1)}, f32[4,17,128]{2,1,0:T(8,128)S(1)}, f32[4,17,17,128]{3,2,1,0:T(8,128)}, f32[4,17,128]{2,1,0:T(8,128)}, /*index=5*/f32[4,17,17,128]{3,2,1,0:T(8,128)S(1)}, s32[]{:T(128)}) while((s32[]{:T(128)}, f32[17,128]{1,0:T(8,128)S(1)}, f32[4,17,128]{2,1,0:T(8,128)S(1)}, ...), condition=%wide.region_32.34_spmd, body=%wide.region_29.33_spmd.sunk | while | flops 145794 | bytes 381533 | solution.py:175
  172.5 4.2 %while.180 = (s32[]{:T(128)}, f32[17,128]{1,0:T(8,128)S(1)}, f32[4,17,128]{2,1,0:T(8,128)S(1)}, f32[4,17,128]{2,1,0:T(8,128)S(1)}, f32[4,17,17,128]{3,2,1,0:T(8,128)}, /*index=5*/s32[]{:T(128)}, s32[]{:T(128)}, s32[]{:T(128)}) while((s32[]{:T(128)}, f32[17,128]{1,0:T(8,128)S(1)}, f32[4,17,128]{2,1,0:T(8,128)S(1)}, ...), condition=%wide.region_35.37_spmd.clone, body=%wide.region_33.36_spmd.clone.sunk | while | flops 78340 | bytes 245879 | solution.py:178
  178.6 3.5 %collective-permute-start.8 = (f32[4,17,16]{2,0,1:T(4,128)}, f32[4,17,16]{2,0,1:T(4,128)}, u32[]{:S(2)}, u32[]{:S(2)}) collective-permute-start(f32[4,17,16]{2,0,1:T(4,128)} %get-tuple-element.1253), channel_id=1, source_target_pairs={{1,0},{2,1},{3,2},{4,3},{5,4},{6,5},{7,6},{0,7},{9,8},{10,9},{11,1... | collective-permute-start | bytes 13064 | tf_op jit(solution)/shard_map/ppermute | solution.py:28
  182.2 2.0 collective-permute-done.7
  185.8 1.8 copy.93
  187.6 3.5 %gather_fusion.1 = f32[512,4,17]{2,1,0:T(4,128)} fusion(f32[4,17,160]{1,0,2:T(4,128)} %copy.93, s32[1024]{0:T(1024)} %copy-done.19), kind=kCustom, calls=%fused_computation.1.clone | custom fusion | bytes 280576 | tf_op jit(solution)/shard_map/jit(_take)/gather | solution.py:162
  191.1 2.2 copy.98
  198.3 3.3 %collective-permute-done.9 = f32[17,128]{1,0:T(8,128)S(1)} collective-permute-done((f32[17,128]{1,0:T(8,128)S(1)}, f32[17,128]{1,0:T(8,128)S(1)}, u32[]{:S(2)}, u32[]{:S(2)}) %collective-permute-start.9) | collective-permute-done | bytes 8736 | tf_op jit(solution)/shard_map/ppermute | solution.py:16
  202.7 8.9 %all_gather.19 = f32[4,17,128]{2,1,0:T(8,128)S(1)} all-gather(f32[1,17,128]{2,1,0:T(8,128)S(1)} %copy.96), channel_id=1, replica_groups=mesh['line'=4,'surf'=8] {'line'}, dimensions={0}, use_global_device_ids=true | all-gather | bytes 43520 | tf_op jit(solution)/shard_map/all_gather | solution.py:174
  211.5 4.4 %while.177 = (s32[]{:T(128)}, f32[17,128]{1,0:T(8,128)S(1)}, f32[4,17,128]{2,1,0:T(8,128)S(1)}, f32[4,17,17,128]{3,2,1,0:T(8,128)}, f32[4,17,128]{2,1,0:T(8,128)S(1)}, /*index=5*/f32[4,17,17,128]{3,2,1,0:T(8,128)S(1)}, s32[]{:T(128)}) while((s32[]{:T(128)}, f32[17,128]{1,0:T(8,128)S(1)}, f32[4,17,128]{2,1,0:T(8,128)S(1)}, ...), condition=%wide.region_51.53_spmd, body=%wide.region_48.52_spmd.sunk | while | flops 145794 | bytes 381533 | solution.py:175
  215.9 4.2 %while.182 = (s32[]{:T(128)}, f32[17,128]{1,0:T(8,128)S(1)}, f32[4,17,128]{2,1,0:T(8,128)S(1)}, f32[4,17,128]{2,1,0:T(8,128)S(1)}, f32[4,17,17,128]{3,2,1,0:T(8,128)}, /*index=5*/s32[]{:T(128)}, s32[]{:T(128)}, s32[]{:T(128)}) while((s32[]{:T(128)}, f32[17,128]{1,0:T(8,128)S(1)}, f32[4,17,128]{2,1,0:T(8,128)S(1)}, ...), condition=%wide.region_54.56_spmd.clone, body=%wide.region_52.55_spmd.clone.sunk | while | flops 78340 | bytes 245879 | solution.py:178
  (1041 shorter events, 120.4 us)
Async XLA Ops:
  0.0 16.7 %copy-start.5 = (f32[4,17,17,128]{3,0,2,1:T(4,128)S(1)}, f32[4,17,17,128]{3,0,2,1:T(4,128)}, u32[]{:S(2)}) copy-start(f32[4,17,17,128]{3,0,2,1:T(4,128)} %param.40) | copy-start | bytes 1775620
  0.0 16.6 %copy-start.17 = (f32[4,17,128]{2,0,1:T(4,128)S(1)}, f32[4,17,128]{2,0,1:T(4,128)}, u32[]{:S(2)}) copy-start(f32[4,17,128]{2,0,1:T(4,128)} %param.42) | copy-start | bytes 104452
  0.8 16.8 %collective-permute-start = (f32[128]{0:T(128)S(1)}, f32[128]{0:T(128)S(1)}, u32[]{:S(2)}, u32[]{:S(2)}) collective-permute-start(f32[128]{0:T(128)S(1)} %slice_bitcast_fusion.44), channel_id=1, source_target_pairs={{0,8},{8,16},{16,24},{1,9},{9,17},{17,25},{2,10},{10,18},{18,26},{... | collective-permute-start | bytes 1544 | tf_op jit(solution)/shard_map/ppermute | solution.py:16
  6.8 10.7 %copy-start.20 = (f32[4,128]{1,0:T(4,128)S(1)}, f32[4,128]{1,0:T(4,128)}, u32[]{:S(2)}) copy-start(f32[4,128]{1,0:T(4,128)} %param.39) | copy-start | bytes 6148
  6.8 10.7 %copy-start.22 = (s32[128]{0:T(128)S(1)}, s32[128]{0:T(128)}, u32[]{:S(2)}) copy-start(s32[128]{0:T(128)} %param.47) | copy-start | bytes 1540
  6.8 10.8 %copy-start.10 = (f32[4,17,128]{2,0,1:T(4,128)S(1)}, f32[4,17,128]{2,0,1:T(4,128)}, u32[]{:S(2)}) copy-start(f32[4,17,128]{2,0,1:T(4,128)} %param.45) | copy-start | bytes 104452
  6.9 13.8 %collective-permute-start.1 = (f32[17,17,128]{2,0,1:T(8,128)S(1)}, f32[17,17,128]{2,0,1:T(8,128)S(1)}, u32[]{:S(2)}, u32[]{:S(2)}) collective-permute-start(f32[17,17,128]{2,0,1:T(8,128)S(1)} %bitcast.930), channel_id=1, source_target_pairs={{0,8},{8,16},{16,24},{1,9},{9,17},{17,25},{2,10},{10,18},{18,26},{... | collective-permute-start | bytes 443912 | tf_op jit(solution)/shard_map/ppermute | solution.py:16
  11.2 6.4 %collective-permute-start.2 = (f32[4,17,16]{2,0,1:T(4,128)S(1)}, f32[4,17,16]{2,0,1:T(4,128)S(1)}, u32[]{:S(2)}, u32[]{:S(2)}) collective-permute-start(f32[4,17,16]{2,0,1:T(4,128)S(1)} %get-tuple-element.1258), channel_id=1, source_target_pairs={{0,1},{1,2},{2,3},{3,4},{4,5},{5,6},{6,7},{7,0},{8,9},{9,10},{10,1... | collective-permute-start | bytes 13064 | tf_op jit(solution)/shard_map/ppermute | solution.py:25
  11.3 6.3 %collective-permute-start.3 = (f32[4,17,16]{2,0,1:T(4,128)S(1)}, f32[4,17,16]{2,0,1:T(4,128)S(1)}, u32[]{:S(2)}, u32[]{:S(2)}) collective-permute-start(f32[4,17,16]{2,0,1:T(4,128)S(1)} %get-tuple-element.1259), channel_id=1, source_target_pairs={{1,0},{2,1},{3,2},{4,3},{5,4},{6,5},{7,6},{0,7},{9,8},{10,9},{11,1... | collective-permute-start | bytes 13064 | tf_op jit(solution)/shard_map/ppermute | solution.py:28
  15.6 4.9 %copy-start.18 = (f32[4,128]{1,0:T(4,128)}, f32[4,128]{1,0:T(4,128)S(1)}, u32[]{:S(2)}) copy-start(f32[4,128]{1,0:T(4,128)S(1)} %get-tuple-element.1266) | copy-start | bytes 6148
  15.6 4.9 %copy-start.21 = (pred[4,128]{1,0:T(4,128)(4,1)}, pred[4,128]{1,0:T(4,128)(4,1)S(1)}, u32[]{:S(2)}) copy-start(pred[4,128]{1,0:T(4,128)(4,1)S(1)} %get-tuple-element.1099) | copy-start | bytes 1540
  56.2 3.5 %copy-start.12 = (f32[3,17,128]{2,1,0:T(8,128)}, f32[3,17,128]{2,1,0:T(8,128)S(1)}, u32[]{:S(2)}) copy-start(f32[3,17,128]{2,1,0:T(8,128)S(1)} %get-tuple-element.819) | copy-start | bytes 78340
  58.4 34.9 %collective-permute-start.6 = (f32[17,128]{1,0:T(8,128)}, f32[17,128]{1,0:T(8,128)}, u32[]{:S(2)}, u32[]{:S(2)}) collective-permute-start(f32[17,128]{1,0:T(8,128)} %get-tuple-element.1257), channel_id=1, source_target_pairs={{8,0},{16,8},{24,16},{9,1},{17,9},{25,17},{10,2},{18,10},{26,18},{... | collective-permute-start | bytes 26120 | tf_op jit(solution)/shard_map/ppermute | solution.py:16
  68.7 3.7 %copy-start.9 = (f32[17,17,128]{2,1,0:T(8,128)S(1)}, f32[17,17,128]{2,1,0:T(8,128)}, u32[]{:S(2)}) copy-start(f32[17,17,128]{2,1,0:T(8,128)} %slice_bitcast_fusion.35) | copy-start | bytes 443908
  69.9 33.2 %collective-permute-start.4 = (f32[17,17,128]{2,1,0:T(8,128)S(1)}, f32[17,17,128]{2,1,0:T(8,128)S(1)}, u32[]{:S(2)}, u32[]{:S(2)}) collective-permute-start(f32[17,17,128]{2,1,0:T(8,128)S(1)} %get-tuple-element.1247), channel_id=1, source_target_pairs={{8,0},{16,8},{24,16},{9,1},{17,9},{25,17},{10,2},{18,10},{26,18},{... | collective-permute-start | bytes 443912 | tf_op jit(solution)/shard_map/ppermute | solution.py:16
  71.2 31.9 %collective-permute-start.5 = (f32[17,17,128]{2,1,0:T(8,128)S(1)}, f32[17,17,128]{2,1,0:T(8,128)S(1)}, u32[]{:S(2)}, u32[]{:S(2)}) collective-permute-start(f32[17,17,128]{2,1,0:T(8,128)S(1)} %get-tuple-element.1245), channel_id=1, source_target_pairs={{8,0},{16,8},{24,16},{9,1},{17,9},{25,17},{10,2},{18,10},{26,18},{... | collective-permute-start | bytes 443912 | tf_op jit(solution)/shard_map/ppermute | solution.py:16
  73.0 21.2 %copy-start.16 = (f32[17,128]{1,0:T(8,128)S(1)}, f32[17,128]{1,0:T(8,128)}, u32[]{:S(2)}) copy-start(f32[17,128]{1,0:T(8,128)} %multiply_reduce_fusion.19) | copy-start | bytes 26116
  73.1 30.1 %copy-start.8 = (f32[17,17,128]{2,1,0:T(8,128)S(1)}, f32[17,17,128]{2,1,0:T(8,128)}, u32[]{:S(2)}) copy-start(f32[17,17,128]{2,1,0:T(8,128)} %slice_bitcast_fusion.34) | copy-start | bytes 443908
  165.4 7.1 %copy-start.11 = (f32[17,128]{1,0:T(8,128)S(1)}, f32[17,128]{1,0:T(8,128)}, u32[]{:S(2)}) copy-start(f32[17,128]{1,0:T(8,128)} %custom-call.2) | copy-start | bytes 26116
  178.6 14.7 %copy-start.7 = (f32[4,4,17,128]{3,1,2,0:T(4,128)S(1)}, f32[4,4,17,128]{3,1,2,0:T(4,128)}, u32[]{:S(2)}) copy-start(f32[4,4,17,128]{3,1,2,0:T(4,128)} %param.43) | copy-start | bytes 417796
  178.6 5.6 %collective-permute-start.7 = (f32[4,17,16]{2,0,1:T(4,128)}, f32[4,17,16]{2,0,1:T(4,128)}, u32[]{:S(2)}, u32[]{:S(2)}) collective-permute-start(f32[4,17,16]{2,0,1:T(4,128)} %get-tuple-element.1252), channel_id=1, source_target_pairs={{0,1},{1,2},{2,3},{3,4},{4,5},{5,6},{6,7},{7,0},{8,9},{9,10},{10,1... | collective-permute-start | bytes 13064 | tf_op jit(solution)/shard_map/ppermute | solution.py:25
  178.6 5.6 %collective-permute-start.8 = (f32[4,17,16]{2,0,1:T(4,128)}, f32[4,17,16]{2,0,1:T(4,128)}, u32[]{:S(2)}, u32[]{:S(2)}) collective-permute-start(f32[4,17,16]{2,0,1:T(4,128)} %get-tuple-element.1253), channel_id=1, source_target_pairs={{1,0},{2,1},{3,2},{4,3},{5,4},{6,5},{7,6},{0,7},{9,8},{10,9},{11,1... | collective-permute-start | bytes 13064 | tf_op jit(solution)/shard_map/ppermute | solution.py:28
  196.1 5.6 %collective-permute-start.9 = (f32[17,128]{1,0:T(8,128)S(1)}, f32[17,128]{1,0:T(8,128)S(1)}, u32[]{:S(2)}, u32[]{:S(2)}) collective-permute-start(f32[17,128]{1,0:T(8,128)S(1)} %get-tuple-element.1255), channel_id=1, source_target_pairs={{8,0},{16,8},{24,16},{9,1},{17,9},{25,17},{10,2},{18,10},{26,18},{... | collective-permute-start | bytes 26120 | tf_op jit(solution)/shard_map/ppermute | solution.py:16
  211.5 8.6 %copy-start.1 = (f32[3,17,17,128]{3,2,1,0:T(8,128)S(1)}, f32[3,17,17,128]{3,2,1,0:T(8,128)}, u32[]{:S(2)}) copy-start(f32[3,17,17,128]{3,2,1,0:T(8,128)} %get-tuple-element.822) | copy-start | bytes 1331716
  (10 other events, 24.0 us)
where the time goes:
time: 223 us; the launch traced here: 221 us
  other arithmetic  92.4 us (41%)
  blocking collectives  61.7 us (28%)
  local copies, waits for them, and re-layouts  33.9 us (15%)
  starting transfers between devices  20.5 us (9%)
  loops' own time  6.24 us (3%)
  waiting for transfers between devices  5.37 us (2%)
    reduce_sum x46, other arithmetic, matrix_vector(): return jnp.sum(matrix_left * vector_right[None, :, :], axis=1)  21.3 us
    all_gather x1, blocking collectives, on_device(): lax.all_gather(red_lower[None], 'line', axis=0, tiled=True)  20.1 us
    all_gather x2, blocking collectives, on_device(): all_right = lax.all_gather(red_right[None], 'line', axis=0, tiled=True)  16.9 us
    all_gather x1, blocking collectives, on_device(): lax.all_gather(red_diag[None], 'line', axis=0, tiled=True)  13.5 us
    ppermute x6, starting transfers between devices, from_behind(): lax.ppermute(value, axis, [(source, source + steps) for source in range(i...  13.4 us
    all_gather x1, blocking collectives, on_device(): lax.all_gather(red_upper[None], 'line', axis=0, tiled=True)  11.2 us
    select_n x49, other arithmetic, invert(): jnp.where(is_pivot, row_result[None], result - factors[:, None, :] * row_...  10.6 us
    select_n x77, other arithmetic, invert(): jnp.where(is_pivot, row_work[None], working - factors[:, None, :] * row_w...  10.5 us
  transfers between devices with their start and end apart: 10, of which 2 were waited for; matrix products, arithmetic and copies ran while one was open for 10% of the time, Pallas kernels for 0%

commit v1 on v0

v1 whole, which is shorter than its diff:
```python
import functools

import jax
import jax.numpy as jnp
from jax import lax
from jax.experimental import pallas as pl
from jax.experimental.pallas import tpu as pltpu
from jax.sharding import PartitionSpec as P

ITERS = 2
MESH = pl.DeviceIdType.MESH

wall_levels = (0.5, 4.0, 32.0)


def groups(width, size=6):
    return [range(s, min(s + size, width)) for s in range(0, width, size)]


def product(out, left, right, base=None):
    width = left.shape[0]
    for rows in groups(width):
        acc = [None] * len(rows)
        for j in range(width):
            line = right[j]
            for n, k in enumerate(rows):
                term = left[k, j : j + 1, :] * line
                acc[n] = term if acc[n] is None else acc[n] + term
        for n, k in enumerate(rows):
            out[k] = acc[n] if base is None else base[k] - acc[n]


def invert_in_place(a):
    width = a.shape[0]
    ids = lax.broadcasted_iota(jnp.int32, a.shape[1:], 0)

    def pivot(k, carry):
        inv = 1.0 / a[k, pl.ds(k, 1), :]
        scaled = a[k] * inv
        here = ids == k
        row = jnp.where(here, inv, scaled)
        update = jnp.where(here, 1.0 + inv, scaled)
        for i in range(width):
            a[i] = a[i] - a[i, pl.ds(k, 1), :] * update
        a[k] = row
        return carry

    lax.fori_loop(0, width, pivot, 0)


def matvec(columns, vector):
    width = columns.shape[0]
    parts = [None] * 3
    for j in range(width):
        term = columns[j] * vector[j : j + 1, :]
        parts[j % 3] = term if parts[j % 3] is None else parts[j % 3] + term
    return parts[0] + parts[1] + parts[2]


def kernel(
    n_line, n_surf,
    win, wout, diag, couple, rhs, start, neighbours,
    out,
    dinv, coup, last, mid_inv, work, mat_in, vec_in, x_in, halo, prev, vecs, right, rprime, send_vec, onehot,
    mat_send, mat_recv, vec_send, vec_recv, x_send, x_recv, halo_send, halo_recv,
):
    cells, width, _, lines = diag.shape
    half = n_line // 2
    me = lax.axis_index("line")
    surf = lax.axis_index("surf")
    lower = me < half
    depth = jnp.where(lower, me, n_line - 1 - me)
    inner = jnp.where(lower, me + 1, me - 1)
    outer = jnp.where(lower, lax.rem(me + n_line - 1, n_line), lax.rem(me + 1, n_line))
    is_mid = depth == half - 1
    not_end = depth > 0
    before = lax.rem(surf + n_surf - 1, n_surf)
    after = lax.rem(surf + 1, n_surf)

    barrier = pltpu.get_barrier_semaphore()
    for peer in (inner, outer):
        pl.semaphore_signal(barrier, inc=1, device_id=(peer, surf), device_id_type=MESH)
    for peer in (before, after):
        pl.semaphore_signal(barrier, inc=1, device_id=(me, peer), device_id_type=MESH)
    pl.semaphore_wait(barrier, 4)

    def remote(src, dst, send, recv, device):
        return pltpu.make_async_remote_copy(
            src_ref=src, dst_ref=dst, send_sem=send, recv_sem=recv,
            device_id=device, device_id_type=MESH,
        )

    def halos(src, sweep):
        return (
            remote(src, halo.at[sweep, 0], halo_send.at[sweep, 0], halo_recv.at[sweep, 0], (me, after)),
            remote(src, halo.at[sweep, 1], halo_send.at[sweep, 1], halo_recv.at[sweep, 1], (me, before)),
        )

    first_halos = halos(start, 0)
    for copy in first_halos:
        copy.start()

    source = lax.broadcasted_iota(jnp.int32, (lines, lines), 0)
    own = surf * lines
    for n in range(4):
        onehot[n] = (neighbours[n : n + 1, :] == source + own).astype(jnp.float32)
    onehot[4] = (neighbours[2:3, :] == source + before * lines).astype(jnp.float32)
    onehot[5] = (neighbours[3:4, :] == source + after * lines).astype(jnp.float32)

    mats = remote(last, mat_in.at[0], mat_send.at[0], mat_recv.at[0], (inner, surf))
    mats_mid = remote(last, mat_in.at[1], mat_send.at[1], mat_recv.at[1], (inner, surf))

    @pl.when(not_end)
    def _():
        mats.wait_recv()

    @pl.when(depth == 0)
    def _():
        mat_in[0] = jnp.zeros_like(mat_in[0])

    last[...] = mat_in[0]

    def factor(t, carry):
        product(work, last, win.at[t], diag.at[t])
        dinv[t] = work[...]
        invert_in_place(dinv.at[t])
        product(last, wout.at[t], dinv.at[t])
        coup[t] = last[...]
        return carry

    lax.fori_loop(0, cells, factor, 0)

    @pl.when(jnp.logical_not(is_mid))
    def _():
        mats.start()
        mats.wait_send()

    @pl.when(is_mid)
    def _():
        mats_mid.start()
        mats_mid.wait()
        product(mid_inv, mat_in.at[1], wout.at[cells - 1], work)
        invert_in_place(mid_inv)

    for sweep in range(ITERS):
        if sweep == 0:
            values, copies = start, first_halos
        else:
            values, copies = prev, halos(prev, sweep)
            for copy in copies:
                copy.start()

        def select(vals, which):
            return lax.dot_general(
                vals, onehot[which], (((1,), (0,)), ((), ())),
                precision=lax.Precision.HIGHEST, preferred_element_type=jnp.float32,
            )

        for t in range(cells):
            vals = values[t]
            right[t] = rhs[t] + sum(couple[t, n] * select(vals, n) for n in range(4))
        for copy in copies:
            copy.wait()
        for t in range(cells):
            right[t] = (
                right[t]
                + couple[t, 2] * select(halo[sweep, 0, t], 4)
                + couple[t, 3] * select(halo[sweep, 1, t], 5)
            )

        vec = remote(send_vec, vec_in.at[sweep, 0], vec_send.at[sweep, 0], vec_recv.at[sweep, 0], (inner, surf))
        vec_mid = remote(send_vec, vec_in.at[sweep, 1], vec_send.at[sweep, 1], vec_recv.at[sweep, 1], (inner, surf))

        @pl.when(depth == 0)
        def _():
            vec_in[sweep, 0] = jnp.zeros((width, lines), jnp.float32)

        @pl.when(not_end)
        def _():
            vec.wait_recv()

        send_vec[...] = vec_in[sweep, 0]

        def forward(t, carry):
            rprime[...] = right[t] - matvec(win.at[t], send_vec)
            value = matvec(dinv.at[t], rprime)
            vecs[t] = value
            send_vec[...] = value
            return carry

        lax.fori_loop(0, cells, forward, 0)

        back = remote(vecs.at[0], x_in.at[sweep], x_send.at[sweep], x_recv.at[sweep], (outer, surf))

        @pl.when(jnp.logical_not(is_mid))
        def _():
            vec.start()
            vec.wait_send()
            back.wait_recv()
            vecs[cells - 1] = vecs[cells - 1] - matvec(coup.at[cells - 1], x_in.at[sweep])

        @pl.when(is_mid)
        def _():
            vec_mid.start()
            vec_mid.wait()
            rprime[...] = rprime[...] - matvec(wout.at[cells - 1], vec_in.at[sweep, 1])
            vecs[cells - 1] = matvec(mid_inv, rprime)

        def backward(s, carry):
            t = cells - 2 - s
            vecs[t] = vecs[t] - matvec(coup.at[t], vecs.at[t + 1])
            return carry

        lax.fori_loop(0, cells - 1, backward, 0)

        @pl.when(not_end)
        def _():
            back.start()
            back.wait_send()

        target = out if sweep == ITERS - 1 else prev
        for t in range(cells):
            target[t] = vecs[t]


def on_device(
    face_coef, face_mix, cell_mix, time_term, couple, rhs, start_delta, neighbours, wall_type
):
    cells, width, _, lines = face_mix.shape
    n_line, n_surf = lax.axis_size("line"), lax.axis_size("surf")
    identity = jnp.eye(width, dtype=jnp.float32)[None, :, :, None]
    place = lax.axis_index("line")
    is_first = (place == 0).astype(jnp.float32)
    wall_term = jnp.zeros(wall_type.shape, jnp.float32)
    for wall_kind, wall_value in enumerate(wall_levels):
        wall_term = wall_term + jnp.where(wall_type == wall_kind, wall_value, 0.0)
    below_coef, below_mix = lax.ppermute(
        (face_coef[-1], face_mix[-1]), "line", [(i, i + 1) for i in range(n_line - 1)]
    )
    coef_below = jnp.concatenate([below_coef[None], face_coef[:-1]], 0)
    mix_below = jnp.concatenate([below_mix[None], face_mix[:-1]], 0)
    coef_diag = (coef_below + face_coef).at[0].add(is_first * wall_term)
    extra = time_term + jnp.sum(couple, axis=1) + coef_diag[:, None]
    cell_t = jnp.swapaxes(cell_mix, 1, 2)
    diag_t = identity * extra[:, None] + cell_t - cell_mix
    lower_t = -coef_below[:, None, None] * identity - mix_below
    upper_t = -face_coef[:, None, None] * identity + jnp.swapaxes(face_mix, 1, 2)
    low = place < n_line // 2
    win = jnp.where(low, lower_t, upper_t[::-1])
    wout = jnp.where(low, upper_t, lower_t[::-1])

    def order(array):
        return jnp.where(low, array, array[::-1])

    f32 = jnp.float32
    mat = (width, width, lines)
    vec = (width, lines)
    dma = pltpu.SemaphoreType.DMA
    vmem = pl.BlockSpec(memory_space=pltpu.VMEM)
    solved = pl.pallas_call(
        functools.partial(kernel, n_line, n_surf),
        out_shape=jax.ShapeDtypeStruct((cells,) + vec, f32),
        in_specs=[vmem] * 7,
        out_specs=vmem,
        scratch_shapes=[
            pltpu.VMEM((cells,) + mat, f32),
            pltpu.VMEM((cells,) + mat, f32),
            pltpu.VMEM(mat, f32),
            pltpu.VMEM(mat, f32),
            pltpu.VMEM(mat, f32),
            pltpu.VMEM((2,) + mat, f32),
            pltpu.VMEM((ITERS, 2) + vec, f32),
            pltpu.VMEM((ITERS,) + vec, f32),
            pltpu.VMEM((ITERS, 2, cells) + vec, f32),
            pltpu.VMEM((cells,) + vec, f32),
            pltpu.VMEM((cells,) + vec, f32),
            pltpu.VMEM((cells,) + vec, f32),
            pltpu.VMEM(vec, f32),
            pltpu.VMEM(vec, f32),
            pltpu.VMEM((6, lines, lines), f32),
            dma((2,)), dma((2,)),
            dma((ITERS, 2)), dma((ITERS, 2)),
            dma((ITERS,)), dma((ITERS,)),
            dma((ITERS, 2)), dma((ITERS, 2)),
        ],
        compiler_params=pltpu.CompilerParams(
            collective_id=0, has_side_effects=True, vmem_limit_bytes=40 * 1024 * 1024
        ),
    )(win, wout, order(diag_t), order(couple), order(rhs), order(start_delta), neighbours)
    return order(solved)


def solution(mesh):
    placed = (
        P("line", "surf"),
        P("line", None, None, "surf"),
        P("line", None, None, "surf"),
        P("line", None, "surf"),
        P("line", None, None, "surf"),
        P("line", None, "surf"),
        P("line", None, "surf"),
        P(None, "surf"),
        P("surf"),
    )
    return jax.shard_map(
        on_device, mesh=mesh, in_specs=placed, out_specs=P("line", None, "surf"), check_vma=False
    )
```

time: 223 us -> 64.6 us (0.29)
  other arithmetic: 92.4 us -> 0.82 us
  blocking collectives: 61.7 us -> 0 us
  Pallas kernels: 0 us -> 47 us
  local copies, waits for them, and re-layouts: 33.9 us -> 6.16 us
  starting transfers between devices: 20.5 us -> 8.37 us
  loops' own time: 6.24 us -> 0 us
  waiting for transfers between devices: 5.37 us -> 1.62 us
    all_gather x5 -> x0, blocking collectives: 61.7 us -> none  [the longest x1 20.1 us: on_device(): lax.all_gather(red_lower[None], 'line', axis=0, tiled=True)]
    pallas_call x0 -> x1, Pallas kernels: none -> 47 us  [on_device(): pl.pallas_call(functools.partial(kernel, n_line, n_surf), out_shape=jax.S...]
    reduce_sum x71 -> x1, other arithmetic: 32.3 us -> 0.09 us  [on_device(): extra = time_term + jnp.sum(couple, axis=1) + coef_diag[:, None]]
    select_n x126 -> x5, other arithmetic: 21.1 us -> 0.3 us  [the longest x1 0.21 us: on_device(): win = jnp.where(low, lower_t, upper_t[::-1])]
    ppermute x10 -> x2, starting transfers between devices: 20.5 us -> 8.37 us  [on_device(): lax.ppermute((face_coef[-1], face_mix[-1]), 'line', [(i, i + 1) for i in...]
    dynamic_update_slice x24 -> x0, other arithmetic: 11.6 us -> none  [the longest x4 6.25 us: on_device(): lax.scan(chain_factor, zero_matrix, (all_lower, all_diag, all_upper))]
    sub x29 -> x1, other arithmetic: 10.9 us -> 0.27 us  [on_device(): diag_t = identity * extra[:, None] + cell_t - cell_mix]
    mul x19 -> x0, local copies, waits for them, and re-layouts: 9.99 us -> none  [the longest x17 9.38 us: matrix_product(): matrix_left[:, :, None, :] * matrix_right[None, :, :, :]]
  transfers between devices with their start and end apart: 10 -> 2, of which waited for: 2 -> 1; matrix products, arithmetic and copies ran while one was open for 10% -> 3% of each run, Pallas kernels for 0% -> 0%
where the time goes in v1:
time: 64.6 us; the launch traced here: 64.3 us
  Pallas kernels  47 us (73%)
  starting transfers between devices  8.37 us (13%)
  local copies, waits for them, and re-layouts  6.16 us (10%)
  waiting for transfers between devices  1.62 us (3%)
  other arithmetic  0.82 us (1%)
    pallas_call x1, Pallas kernels, on_device(): pl.pallas_call(functools.partial(kernel, n_line, n_surf), out_shape=jax.S...  47 us
    ppermute x2, starting transfers between devices, on_device(): lax.ppermute((face_coef[-1], face_mix[-1]), 'line', [(i, i + 1) for i in...  8.37 us
    unnamed x23, local copies, waits for them, and re-layouts  3.59 us
    ppermute x2, waiting for transfers between devices, on_device(): lax.ppermute((face_coef[-1], face_mix[-1]), 'line', [(i, i + 1) for i in...  1.62 us
  transfers between devices with their start and end apart: 2, of which 1 were waited for; matrix products, arithmetic and copies ran while one was open for 3% of the time, Pallas kernels for 0%

profile of v1, /device:TPU:0, one launch (start us, length us, event | category | flops | bytes accessed | tf_op | source)
XLA Modules:
  0.0 64.3 jit_solution(4795213426904666315)
XLA Ops:
  0.0 0.7 %slice_bitcast_fusion = f32[128]{0:T(128)S(1)} fusion(f32[4,128]{1,0:T(4,128)} %param.11), kind=kLoop, calls=%fused_computation.27 | loop fusion | bytes 1024 | tf_op jit(solution)/shard_map/squeeze | solution.py:238
  0.7 4.8 %collective-permute-start = (f32[128]{0:T(128)S(1)}, f32[128]{0:T(128)S(1)}, u32[]{:S(2)}, u32[]{:S(2)}) collective-permute-start(f32[128]{0:T(128)S(1)} %slice_bitcast_fusion), channel_id=1, source_target_pairs={{0,8},{8,16},{16,24},{1,9},{9,17},{17,25},{2,10},{10,18},{18,26},{... | collective-permute-start | bytes 1544 | tf_op jit(solution)/shard_map/ppermute | solution.py:237
  5.5 1.2 %slice.31 = f32[1,17,17,128]{3,0,2,1:T(1,128)S(1)} slice(f32[4,17,17,128]{3,0,2,1:T(4,128)} %param.12), slice={[3:4], [0:17], [0:17], [0:128]} | slice | bytes 295936 | tf_op jit(solution)/shard_map/slice | solution.py:238
  6.7 0.0 copy-start.3
  6.8 0.0 copy-start.4
  6.8 0.0 copy-start.5
  6.8 0.0 copy-start.1
  6.8 3.5 %collective-permute-start.1 = (f32[17,17,128]{2,1,0:T(8,128)S(1)}, f32[17,17,128]{2,1,0:T(8,128)S(1)}, u32[]{:S(2)}, u32[]{:S(2)}) collective-permute-start(f32[17,17,128]{2,1,0:T(8,128)S(1)} %bitcast.23), channel_id=1, source_target_pairs={{0,8},{8,16},{16,24},{1,9},{9,17},{17,25},{2,10},{10,18},{18,26},{... | collective-permute-start | bytes 443912 | tf_op jit(solution)/shard_map/ppermute | solution.py:237
  10.5 0.1 copy.37
  10.6 0.1 reduce_sum.9
  10.7 0.0 copy-start.7
  10.7 0.7 %copy-done.7 = f32[4,128]{1,0:T(4,128)S(1)} copy-done((f32[4,128]{1,0:T(4,128)S(1)}, f32[4,128]{1,0:T(4,128)}, u32[]{:S(2)}) %copy-start.7) | copy-done | bytes 2072
  11.4 0.6 %copy-done.8 = s32[128]{0:T(128)S(1)} copy-done((s32[128]{0:T(128)S(1)}, s32[128]{0:T(128)}, u32[]{:S(2)}) %copy-start.8) | copy-done | bytes 536
  12.1 0.1 bitcast_add_fusion.1
  12.2 0.6 copy-done.6
  12.9 1.6 %collective-permute-done.1 = f32[17,17,128]{2,1,0:T(8,128)S(1)} collective-permute-done((f32[17,17,128]{2,1,0:T(8,128)S(1)}, f32[17,17,128]{2,1,0:T(8,128)S(1)}, u32[]{:S(2)}, u32[]{:S(2)}) %collective-permute-start.1) | collective-permute-done | bytes 148000 | tf_op jit(solution)/shard_map/ppermute | solution.py:237
  14.5 0.2 reverse_select_fusion.2
  14.7 0.8 %copy-done.2 = f32[4,17,17,128]{3,0,2,1:T(4,128)S(1)} copy-done((f32[4,17,17,128]{3,0,2,1:T(4,128)S(1)}, f32[4,17,17,128]{3,0,2,1:T(4,128)}, u32[]{:S(2)}) %copy-start.2) | copy-done | bytes 591896
  15.6 0.3 fusion
  15.8 0.1 reverse_select_fusion.diag
  15.9 0.0 copy-start
  15.9 0.7 %copy-done = s32[4,128]{1,0:T(4,128)S(1)} copy-done((s32[4,128]{1,0:T(4,128)S(1)}, s32[4,128]{1,0:T(4,128)}, u32[]{:S(2)}) %copy-start) | copy-done | bytes 2072
  16.6 47.0 %shard_map.91 = f32[4,17,128]{2,1,0:T(8,128)S(1)} custom-call(f32[4,17,17,128]{3,2,1,0:T(8,128)S(1)} %get-tuple-element.17.win, f32[4,17,17,128]{3,2,1,0:T(8,128)S(1)} %get-tuple-element.20.wout, f32[4,17,17,128]{3,2,1,0:T(8,128)S(1)} %reverse_select_fusion.diag, f32[4,4,17,128]{3,2,1,0:T(8,128)S(1)} %reverse_select_fusion.3.couple, ...), custom_call_target="tpu_custom_call" | custom-call | tf_op jit(solution)/shard_map/pallas_call | solution.py:260
  63.6 0.6 copy.35
  (20 shorter events, 0.2 us)
Async XLA Ops:
  0.7 10.0 %collective-permute-start = (f32[128]{0:T(128)S(1)}, f32[128]{0:T(128)S(1)}, u32[]{:S(2)}, u32[]{:S(2)}) collective-permute-start(f32[128]{0:T(128)S(1)} %slice_bitcast_fusion), channel_id=1, source_target_pairs={{0,8},{8,16},{16,24},{1,9},{9,17},{17,25},{2,10},{10,18},{18,26},{... | collective-permute-start | bytes 1544 | tf_op jit(solution)/shard_map/ppermute | solution.py:237
  6.7 3.6 %copy-start.3 = (f32[4,4,17,128]{3,1,2,0:T(4,128)S(1)}, f32[4,4,17,128]{3,1,2,0:T(4,128)}, u32[]{:S(2)}) copy-start(f32[4,4,17,128]{3,1,2,0:T(4,128)} %param.15) | copy-start | bytes 417796
  6.8 3.7 %copy-start.4 = (f32[4,17,128]{2,0,1:T(4,128)S(1)}, f32[4,17,128]{2,0,1:T(4,128)}, u32[]{:S(2)}) copy-start(f32[4,17,128]{2,0,1:T(4,128)} %param.17) | copy-start | bytes 104452
  6.8 3.7 %copy-start.5 = (f32[4,17,128]{2,0,1:T(4,128)S(1)}, f32[4,17,128]{2,0,1:T(4,128)}, u32[]{:S(2)}) copy-start(f32[4,17,128]{2,0,1:T(4,128)} %param.16) | copy-start | bytes 104452
  6.8 3.7 %copy-start.1 = (f32[4,17,17,128]{3,0,2,1:T(4,128)S(1)}, f32[4,17,17,128]{3,0,2,1:T(4,128)}, u32[]{:S(2)}) copy-start(f32[4,17,17,128]{3,0,2,1:T(4,128)} %param.12) | copy-start | bytes 1775620
  6.8 7.7 %collective-permute-start.1 = (f32[17,17,128]{2,1,0:T(8,128)S(1)}, f32[17,17,128]{2,1,0:T(8,128)S(1)}, u32[]{:S(2)}, u32[]{:S(2)}) collective-permute-start(f32[17,17,128]{2,1,0:T(8,128)S(1)} %bitcast.23), channel_id=1, source_target_pairs={{0,8},{8,16},{16,24},{1,9},{9,17},{17,25},{2,10},{10,18},{18,26},{... | collective-permute-start | bytes 443912 | tf_op jit(solution)/shard_map/ppermute | solution.py:237
  10.7 0.7 %copy-start.7 = (f32[4,128]{1,0:T(4,128)S(1)}, f32[4,128]{1,0:T(4,128)}, u32[]{:S(2)}) copy-start(f32[4,128]{1,0:T(4,128)} %param.11) | copy-start | bytes 6148
  11.4 0.7 %copy-start.8 = (s32[128]{0:T(128)S(1)}, s32[128]{0:T(128)}, u32[]{:S(2)}) copy-start(s32[128]{0:T(128)} %param.19) | copy-start | bytes 1540
  12.1 0.8 %copy-start.6 = (f32[4,17,128]{2,0,1:T(4,128)S(1)}, f32[4,17,128]{2,0,1:T(4,128)}, u32[]{:S(2)}) copy-start(f32[4,17,128]{2,0,1:T(4,128)} %param.14) | copy-start | bytes 104452
  14.5 1.1 %copy-start.2 = (f32[4,17,17,128]{3,0,2,1:T(4,128)S(1)}, f32[4,17,17,128]{3,0,2,1:T(4,128)}, u32[]{:S(2)}) copy-start(f32[4,17,17,128]{3,0,2,1:T(4,128)} %param.13) | copy-start | bytes 1775620
  15.9 0.7 %copy-start = (s32[4,128]{1,0:T(4,128)S(1)}, s32[4,128]{1,0:T(4,128)}, u32[]{:S(2)}) copy-start(s32[4,128]{1,0:T(4,128)} %neighbours.1) | copy-start | bytes 6148

commit v2 on v1

--- a/solution.py
+++ b/solution.py
@@ -33,19 +33,18 @@
 def invert_in_place(a):
     width = a.shape[0]
     ids = lax.broadcasted_iota(jnp.int32, a.shape[1:], 0)
-
-    def pivot(k, carry):
-        inv = 1.0 / a[k, pl.ds(k, 1), :]
-        scaled = a[k] * inv
+    rows = [a[i] for i in range(width)]
+    for k in range(width):
+        inv = 1.0 / rows[k][k : k + 1, :]
+        scaled = rows[k] * inv
         here = ids == k
-        row = jnp.where(here, inv, scaled)
         update = jnp.where(here, 1.0 + inv, scaled)
-        for i in range(width):
-            a[i] = a[i] - a[i, pl.ds(k, 1), :] * update
-        a[k] = row
-        return carry
-
-    lax.fori_loop(0, width, pivot, 0)
+        for step in range(1, width):
+            i = (k + step) % width
+            rows[i] = rows[i] - rows[i][k : k + 1, :] * update
+        rows[k] = jnp.where(here, inv, scaled)
+    for i in range(width):
+        a[i] = rows[i]
 
 
 def matvec(columns, vector):
@@ -59,15 +58,18 @@
 
 def kernel(
     n_line, n_surf,
-    win, wout, diag, couple, rhs, start, neighbours,
+    win_own, wout_own, diag_own, top_mat, top_coef, couple, rhs, start, neighbours,
     out,
+    win, wout, diag, edge_mat, edge_coef, edge_send, edge_recv,
     dinv, coup, last, mid_inv, work, mat_in, vec_in, x_in, halo, prev, vecs, right, rprime, send_vec, onehot,
     mat_send, mat_recv, vec_send, vec_recv, x_send, x_recv, halo_send, halo_recv,
 ):
-    cells, width, _, lines = diag.shape
+    cells, width, _, lines = diag_own.shape
     half = n_line // 2
     me = lax.axis_index("line")
     surf = lax.axis_index("surf")
+    above = lax.rem(me + 1, n_line)
+    below = lax.rem(me + n_line - 1, n_line)
     lower = me < half
     depth = jnp.where(lower, me, n_line - 1 - me)
     inner = jnp.where(lower, me + 1, me - 1)
@@ -78,7 +80,7 @@
     after = lax.rem(surf + 1, n_surf)
 
     barrier = pltpu.get_barrier_semaphore()
-    for peer in (inner, outer):
+    for peer in (above, below):
         pl.semaphore_signal(barrier, inc=1, device_id=(peer, surf), device_id_type=MESH)
     for peer in (before, after):
         pl.semaphore_signal(barrier, inc=1, device_id=(me, peer), device_id_type=MESH)
@@ -99,6 +101,16 @@
     first_halos = halos(start, 0)
     for copy in first_halos:
         copy.start()
+
+    edge_copies = (
+        remote(top_mat, edge_mat, edge_send.at[0], edge_recv.at[0], (above, surf)),
+        remote(top_coef, edge_coef, edge_send.at[1], edge_recv.at[1], (above, surf)),
+    )
+
+    @pl.when(me < n_line - 1)
+    def _():
+        for copy in edge_copies:
+            copy.start()
 
     source = lax.broadcasted_iota(jnp.int32, (lines, lines), 0)
     own = surf * lines
@@ -120,7 +132,40 @@
 
     last[...] = mat_in[0]
 
+    edge_step = jnp.where(lower, 0, cells - 1)
+    eye = lax.broadcasted_iota(jnp.int32, (width, lines), 0)
+
+    @pl.when(me == 0)
+    def _():
+        edge_mat[...] = jnp.zeros_like(edge_mat)
+        edge_coef[...] = jnp.zeros_like(edge_coef)
+
     def factor(t, carry):
+        for i in range(width):
+            win[t, i] = win_own[t, i]
+            wout[t, i] = wout_own[t, i]
+            diag[t, i] = diag_own[t, i]
+
+        @pl.when(t == edge_step)
+        def _():
+            @pl.when(me > 0)
+            def _():
+                for copy in edge_copies:
+                    copy.wait_recv()
+
+            for i in range(width):
+                diag[t, i] = diag[t, i] + jnp.where(eye == i, edge_coef[...], 0.0)
+
+            @pl.when(lower)
+            def _():
+                for i in range(width):
+                    win[t, i] = edge_mat[i]
+
+            @pl.when(jnp.logical_not(lower))
+            def _():
+                for i in range(width):
+                    wout[t, i] = edge_mat[i]
+
         product(work, last, win.at[t], diag.at[t])
         dinv[t] = work[...]
         invert_in_place(dinv.at[t])
@@ -129,6 +174,11 @@
         return carry
 
     lax.fori_loop(0, cells, factor, 0)
+
+    @pl.when(me < n_line - 1)
+    def _():
+        for copy in edge_copies:
+            copy.wait_send()
 
     @pl.when(jnp.logical_not(is_mid))
     def _():
@@ -234,16 +284,12 @@
     wall_term = jnp.zeros(wall_type.shape, jnp.float32)
     for wall_kind, wall_value in enumerate(wall_levels):
         wall_term = wall_term + jnp.where(wall_type == wall_kind, wall_value, 0.0)
-    below_coef, below_mix = lax.ppermute(
-        (face_coef[-1], face_mix[-1]), "line", [(i, i + 1) for i in range(n_line - 1)]
-    )
-    coef_below = jnp.concatenate([below_coef[None], face_coef[:-1]], 0)
-    mix_below = jnp.concatenate([below_mix[None], face_mix[:-1]], 0)
-    coef_diag = (coef_below + face_coef).at[0].add(is_first * wall_term)
+    coef_diag = face_coef.at[1:].add(face_coef[:-1]).at[0].add(is_first * wall_term)
     extra = time_term + jnp.sum(couple, axis=1) + coef_diag[:, None]
     cell_t = jnp.swapaxes(cell_mix, 1, 2)
     diag_t = identity * extra[:, None] + cell_t - cell_mix
-    lower_t = -coef_below[:, None, None] * identity - mix_below
+    above_t = -face_coef[:, None, None] * identity - face_mix
+    lower_t = jnp.concatenate([jnp.zeros_like(above_t[:1]), above_t[:-1]], 0)
     upper_t = -face_coef[:, None, None] * identity + jnp.swapaxes(face_mix, 1, 2)
     low = place < n_line // 2
     win = jnp.where(low, lower_t, upper_t[::-1])
@@ -260,9 +306,15 @@
     solved = pl.pallas_call(
         functools.partial(kernel, n_line, n_surf),
         out_shape=jax.ShapeDtypeStruct((cells,) + vec, f32),
-        in_specs=[vmem] * 7,
+        in_specs=[vmem] * 9,
         out_specs=vmem,
         scratch_shapes=[
+            pltpu.VMEM((cells,) + mat, f32),
+            pltpu.VMEM((cells,) + mat, f32),
+            pltpu.VMEM((cells,) + mat, f32),
+            pltpu.VMEM(mat, f32),
+            pltpu.VMEM((1, lines), f32),
+            dma((2,)), dma((2,)),
             pltpu.VMEM((cells,) + mat, f32),
             pltpu.VMEM((cells,) + mat, f32),
             pltpu.VMEM(mat, f32),
@@ -286,7 +338,7 @@
         compiler_params=pltpu.CompilerParams(
             collective_id=0, has_side_effects=True, vmem_limit_bytes=40 * 1024 * 1024
         ),
-    )(win, wout, order(diag_t), order(couple), order(rhs), order(start_delta), neighbours)
+    )(win, wout, order(diag_t), above_t[-1], face_coef[-1:], order(couple), order(rhs), order(start_delta), neighbours)
     return order(solved)
 
 

time: 64.6 us -> 48.8 us (0.76)
  starting transfers between devices: 8.37 us -> 0 us
  Pallas kernels: 47 us -> 42 us
  waiting for transfers between devices: 1.62 us -> 0 us
  local copies, waits for them, and re-layouts: 6.16 us -> 4.82 us
    ppermute x2 -> x0, starting transfers between devices: 8.37 us -> none  [on_device(): lax.ppermute((face_coef[-1], face_mix[-1]), 'line', [(i, i + 1) for i in...]
    pallas_call x1, Pallas kernels: 47 us -> 42 us  [on_device(): pl.pallas_call(functools.partial(kernel, n_line, n_surf), out_shape=jax.S...]
    ppermute x2 -> x0, waiting for transfers between devices: 1.62 us -> none  [on_device(): lax.ppermute((face_coef[-1], face_mix[-1]), 'line', [(i, i + 1) for i in...]
    slice x1 -> x2, local copies, waits for them, and re-layouts: 1.22 us -> 0.05 us  [the longest x1 0.04 us: on_device(): lower_t = jnp.concatenate([jnp.zeros_like(above_t[:1]), above_t[:-1]], 0)]
    squeeze x1, local copies, waits for them, and re-layouts: 0.68 us -> 0.02 us  [on_device(): above_t[-1]]
    unnamed x23 -> x18, local copies, waits for them, and re-layouts: 3.59 us -> 3.98 us
  transfers between devices with their start and end apart: 2 -> 0, of which waited for: 1 -> 0; matrix products, arithmetic and copies ran while one was open for 3% -> 0% of each run, Pallas kernels for 0% -> 0%
where the time goes in v2:
time: 48.8 us; the launch traced here: 48.4 us
  Pallas kernels  42 us (86%)
  local copies, waits for them, and re-layouts  4.82 us (10%)
  other arithmetic  1.44 us (3%)
    pallas_call x1, Pallas kernels, on_device(): pl.pallas_call(functools.partial(kernel, n_line, n_surf), out_shape=jax.S...  42 us
    unnamed x18, local copies, waits for them, and re-layouts  3.98 us

profile of v2, /device:TPU:0, one launch (start us, length us, event | category | flops | bytes accessed | tf_op | source)
XLA Modules:
  0.0 48.4 jit_solution(3350834979164916862)
XLA Ops:
  0.0 0.0 copy-start.4
  0.0 0.7 %copy.46 = f32[4,128]{1,0:T(4,128)S(1)} copy(f32[4,128]{1,0:T(4,128)} %param.13) | data formatting | bytes 4096
  0.7 0.1 scatter-add.6
  0.8 0.7 %fusion.7 = f32[1,128]{1,0:T(1,128)S(1)} fusion(s32[128]{0:T(128)} %param.21, f32[4,128]{1,0:T(4,128)S(1)} %scatter-add.6, f32[]{:T(128)S(6)} %convert_element_type.13), kind=kLoop, calls=%fused_computation.24 | loop fusion | flops 1280 | bytes 1540 | tf_op jit(solution)/shard_map/add | solution.py:287
  1.5 0.0 copy-done.4
  1.5 0.0 copy-start.5
  1.6 0.7 %copy-done.5 = f32[4,17,128]{2,0,1:T(4,128)S(1)} copy-done((f32[4,17,128]{2,0,1:T(4,128)S(1)}, f32[4,17,128]{2,0,1:T(4,128)}, u32[]{:S(2)}) %copy-start.5) | copy-done | bytes 34840
  2.3 0.0 copy-start.3
  2.3 0.0 copy-start.6
  2.3 0.0 copy-start.1
  2.3 0.9 %copy-done.3 = f32[4,4,17,128]{3,1,2,0:T(4,128)S(1)} copy-done((f32[4,4,17,128]{3,1,2,0:T(4,128)S(1)}, f32[4,4,17,128]{3,1,2,0:T(4,128)}, u32[]{:S(2)}) %copy-start.3) | copy-done | bytes 139288
  3.2 0.1 reduce_sum.9
  3.3 0.0 copy-done.6
  3.4 0.1 copy-done.1
  3.5 0.2 multiply_subtract_fusion
  3.7 0.0 copy-start.2
  3.8 0.1 fusion.8
  3.9 0.9 %copy-done.2 = f32[4,17,17,128]{3,0,2,1:T(4,128)S(1)} copy-done((f32[4,17,17,128]{3,0,2,1:T(4,128)S(1)}, f32[4,17,17,128]{3,0,2,1:T(4,128)}, u32[]{:S(2)}) %copy-start.2) | copy-done | bytes 591896
  4.8 0.3 fusion
  5.1 0.0 copy-start
  5.1 0.1 reverse_select_fusion.diag_own
  5.2 0.6 %copy-done = s32[4,128]{1,0:T(4,128)S(1)} copy-done((s32[4,128]{1,0:T(4,128)S(1)}, s32[4,128]{1,0:T(4,128)}, u32[]{:S(2)}) %copy-start) | copy-done | bytes 2072
  5.8 42.0 %shard_map.91 = f32[4,17,128]{2,1,0:T(8,128)S(1)} custom-call(f32[4,17,17,128]{3,2,1,0:T(8,128)S(1)} %get-tuple-element.30.win_own, f32[4,17,17,128]{3,2,1,0:T(8,128)S(1)} %get-tuple-element.34.wout_own, f32[4,17,17,128]{3,2,1,0:T(8,128)S(1)} %reverse_select_fusion.diag_own, f32[17,17,128]{2,1,0:T(8,128)S(1)} %slice_bitcast_fusion.top_mat, ...), custom_call_target="tpu_custom_call" | custom-call | tf_op jit(solution)/shard_map/pallas_call | solution.py:306
  47.8 0.6 %copy.33 = f32[4,17,128]{2,0,1:T(4,128)} copy(f32[4,17,128]{2,1,0:T(8,128)S(1)} %reverse_select_fusion.4) | data formatting | bytes 69632 | tf_op jit(solution)/shard_map/jit(_where)/select_n | solution.py:299
  (14 shorter events, 0.2 us)
Async XLA Ops:
  0.0 1.5 %copy-start.4 = (f32[4,17,128]{2,0,1:T(4,128)S(1)}, f32[4,17,128]{2,0,1:T(4,128)}, u32[]{:S(2)}) copy-start(f32[4,17,128]{2,0,1:T(4,128)} %param.18) | copy-start | bytes 104452
  1.5 0.8 %copy-start.5 = (f32[4,17,128]{2,0,1:T(4,128)S(1)}, f32[4,17,128]{2,0,1:T(4,128)}, u32[]{:S(2)}) copy-start(f32[4,17,128]{2,0,1:T(4,128)} %param.19) | copy-start | bytes 104452
  2.3 0.9 %copy-start.3 = (f32[4,4,17,128]{3,1,2,0:T(4,128)S(1)}, f32[4,4,17,128]{3,1,2,0:T(4,128)}, u32[]{:S(2)}) copy-start(f32[4,4,17,128]{3,1,2,0:T(4,128)} %param.17) | copy-start | bytes 417796
  2.3 1.0 %copy-start.6 = (f32[4,17,128]{2,0,1:T(4,128)S(1)}, f32[4,17,128]{2,0,1:T(4,128)}, u32[]{:S(2)}) copy-start(f32[4,17,128]{2,0,1:T(4,128)} %param.16) | copy-start | bytes 104452
  2.3 1.2 %copy-start.1 = (f32[4,17,17,128]{3,0,2,1:T(4,128)S(1)}, f32[4,17,17,128]{3,0,2,1:T(4,128)}, u32[]{:S(2)}) copy-start(f32[4,17,17,128]{3,0,2,1:T(4,128)} %param.14) | copy-start | bytes 1775620
  3.7 1.1 %copy-start.2 = (f32[4,17,17,128]{3,0,2,1:T(4,128)S(1)}, f32[4,17,17,128]{3,0,2,1:T(4,128)}, u32[]{:S(2)}) copy-start(f32[4,17,17,128]{3,0,2,1:T(4,128)} %param.15) | copy-start | bytes 1775620
  5.1 0.7 %copy-start = (s32[4,128]{1,0:T(4,128)S(1)}, s32[4,128]{1,0:T(4,128)}, u32[]{:S(2)}) copy-start(s32[4,128]{1,0:T(4,128)} %neighbours.1) | copy-start | bytes 6148

commit v3 on v2

--- a/solution.py
+++ b/solution.py
@@ -61,11 +61,12 @@
     win_own, wout_own, diag_own, top_mat, top_coef, couple, rhs, start, neighbours,
     out,
     win, wout, diag, edge_mat, edge_coef, edge_send, edge_recv,
-    dinv, coup, last, mid_inv, work, mat_in, vec_in, x_in, halo, prev, vecs, right, rprime, send_vec, onehot,
+    dinv, coup, last, mid_inv, work, mat_in, vec_in, x_in, halo, prev, vecs, right, rprime, send_vec, onehot, stack, picked,
     mat_send, mat_recv, vec_send, vec_recv, x_send, x_recv, halo_send, halo_recv,
 ):
     cells, width, _, lines = diag_own.shape
     half = n_line // 2
+    rows_each = stack.shape[1] // (3 * cells)
     me = lax.axis_index("line")
     surf = lax.axis_index("surf")
     above = lax.rem(me + 1, n_line)
@@ -114,10 +115,50 @@
 
     source = lax.broadcasted_iota(jnp.int32, (lines, lines), 0)
     own = surf * lines
-    for n in range(4):
-        onehot[n] = (neighbours[n : n + 1, :] == source + own).astype(jnp.float32)
-    onehot[4] = (neighbours[2:3, :] == source + before * lines).astype(jnp.float32)
-    onehot[5] = (neighbours[3:4, :] == source + after * lines).astype(jnp.float32)
+    for n, (slot, base) in enumerate(
+        ((0, own), (1, own), (2, own), (3, own), (2, before * lines), (3, after * lines))
+    ):
+        hits = neighbours[slot : slot + 1, :] == source + base
+        onehot[:, n * lines : (n + 1) * lines] = hits.astype(jnp.float32)
+    for which in range(3):
+        stack[which] = jnp.zeros_like(stack[which])
+
+    def gather(which, values, first, count):
+        pieces = stack.at[which]
+        for t in range(cells):
+            rest = values[t]
+            for q in range(3):
+                piece = rest.astype(jnp.bfloat16).astype(jnp.float32)
+                begin = (q * cells + t) * rows_each
+                pieces[begin : begin + width, :] = piece
+                rest = rest - piece
+        picked[:, first * lines : (first + count) * lines] = jnp.dot(
+            pieces[...].astype(jnp.bfloat16),
+            onehot[:, first * lines : (first + count) * lines].astype(jnp.bfloat16),
+            preferred_element_type=jnp.float32,
+        )
+
+    def chosen(t, n):
+        parts = []
+        for q in range(3):
+            begin = (q * cells + t) * rows_each
+            parts.append(picked[begin : begin + width, n * lines : (n + 1) * lines])
+        return parts[2] + parts[1] + parts[0]
+
+    def form_right(values, copies, sweep):
+        gather(0, values, 0, 4)
+        for copy in copies:
+            copy.wait()
+        gather(1, halo.at[sweep, 0], 4, 1)
+        gather(2, halo.at[sweep, 1], 5, 1)
+        for t in range(cells):
+            total = rhs[t] + couple[t, 0] * chosen(t, 0) + couple[t, 1] * chosen(t, 1)
+            total = total + couple[t, 2] * (chosen(t, 2) + chosen(t, 4))
+            right[t] = total + couple[t, 3] * (chosen(t, 3) + chosen(t, 5))
+
+    @pl.when(not_end)
+    def _():
+        form_right(start, first_halos, 0)
 
     mats = remote(last, mat_in.at[0], mat_send.at[0], mat_recv.at[0], (inner, surf))
     mats_mid = remote(last, mat_in.at[1], mat_send.at[1], mat_recv.at[1], (inner, surf))
@@ -175,15 +216,9 @@
 
     lax.fori_loop(0, cells, factor, 0)
 
-    @pl.when(me < n_line - 1)
-    def _():
-        for copy in edge_copies:
-            copy.wait_send()
-
     @pl.when(jnp.logical_not(is_mid))
     def _():
         mats.start()
-        mats.wait_send()
 
     @pl.when(is_mid)
     def _():
@@ -194,29 +229,14 @@
 
     for sweep in range(ITERS):
         if sweep == 0:
-            values, copies = start, first_halos
+            @pl.when(depth == 0)
+            def _():
+                form_right(start, first_halos, 0)
         else:
-            values, copies = prev, halos(prev, sweep)
+            copies = halos(prev, sweep)
             for copy in copies:
                 copy.start()
-
-        def select(vals, which):
-            return lax.dot_general(
-                vals, onehot[which], (((1,), (0,)), ((), ())),
-                precision=lax.Precision.HIGHEST, preferred_element_type=jnp.float32,
-            )
-
-        for t in range(cells):
-            vals = values[t]
-            right[t] = rhs[t] + sum(couple[t, n] * select(vals, n) for n in range(4))
-        for copy in copies:
-            copy.wait()
-        for t in range(cells):
-            right[t] = (
-                right[t]
-                + couple[t, 2] * select(halo[sweep, 0, t], 4)
-                + couple[t, 3] * select(halo[sweep, 1, t], 5)
-            )
+            form_right(prev, copies, sweep)
 
         vec = remote(send_vec, vec_in.at[sweep, 0], vec_send.at[sweep, 0], vec_recv.at[sweep, 0], (inner, surf))
         vec_mid = remote(send_vec, vec_in.at[sweep, 1], vec_send.at[sweep, 1], vec_recv.at[sweep, 1], (inner, surf))
@@ -271,6 +291,15 @@
         target = out if sweep == ITERS - 1 else prev
         for t in range(cells):
             target[t] = vecs[t]
+
+    @pl.when(me < n_line - 1)
+    def _():
+        for copy in edge_copies:
+            copy.wait_send()
+
+    @pl.when(jnp.logical_not(is_mid))
+    def _():
+        mats.wait_send()
 
 
 def on_device(
@@ -300,6 +329,7 @@
 
     f32 = jnp.float32
     mat = (width, width, lines)
+    pad = (width + 7) // 8 * 8
     vec = (width, lines)
     dma = pltpu.SemaphoreType.DMA
     vmem = pl.BlockSpec(memory_space=pltpu.VMEM)
@@ -329,7 +359,9 @@
             pltpu.VMEM((cells,) + vec, f32),
             pltpu.VMEM(vec, f32),
             pltpu.VMEM(vec, f32),
-            pltpu.VMEM((6, lines, lines), f32),
+            pltpu.VMEM((lines, 6 * lines), f32),
+            pltpu.VMEM((3, 3 * cells * pad, lines), f32),
+            pltpu.VMEM((3 * cells * pad, 6 * lines), f32),
             dma((2,)), dma((2,)),
             dma((ITERS, 2)), dma((ITERS, 2)),
             dma((ITERS,)), dma((ITERS,)),

time: 48.8 us -> 46.7 us (0.957)
  Pallas kernels: 42 us -> 40 us
    pallas_call x1, Pallas kernels: 42 us -> 40 us  [on_device(): pl.pallas_call(functools.partial(kernel, n_line, n_surf), out_shape=jax.S...]
where the time goes in v3:
time: 46.7 us; the launch traced here: 46.4 us
  Pallas kernels  40 us (86%)
  local copies, waits for them, and re-layouts  4.82 us (10%)
  other arithmetic  1.44 us (3%)
    pallas_call x1, Pallas kernels, on_device(): pl.pallas_call(functools.partial(kernel, n_line, n_surf), out_shape=jax.S...  40 us
    unnamed x18, local copies, waits for them, and re-layouts  3.98 us

profile of v3, /device:TPU:0, one launch (start us, length us, event | category | flops | bytes accessed | tf_op | source)
XLA Modules:
  0.0 46.4 jit_solution(6352753400163074564)
XLA Ops:
  0.0 0.0 copy-start.4
  0.0 0.7 %copy.46 = f32[4,128]{1,0:T(4,128)S(1)} copy(f32[4,128]{1,0:T(4,128)} %param.13) | data formatting | bytes 4096
  0.7 0.1 scatter-add.6
  0.8 0.7 %fusion.7 = f32[1,128]{1,0:T(1,128)S(1)} fusion(s32[128]{0:T(128)} %param.21, f32[4,128]{1,0:T(4,128)S(1)} %scatter-add.6, f32[]{:T(128)S(6)} %convert_element_type.13), kind=kLoop, calls=%fused_computation.24 | loop fusion | flops 1280 | bytes 1540 | tf_op jit(solution)/shard_map/add | solution.py:316
  1.5 0.0 copy-done.4
  1.5 0.0 copy-start.5
  1.6 0.7 %copy-done.5 = f32[4,17,128]{2,0,1:T(4,128)S(1)} copy-done((f32[4,17,128]{2,0,1:T(4,128)S(1)}, f32[4,17,128]{2,0,1:T(4,128)}, u32[]{:S(2)}) %copy-start.5) | copy-done | bytes 34840
  2.3 0.0 copy-start.3
  2.3 0.0 copy-start.6
  2.3 0.0 copy-start.1
  2.3 0.9 %copy-done.3 = f32[4,4,17,128]{3,1,2,0:T(4,128)S(1)} copy-done((f32[4,4,17,128]{3,1,2,0:T(4,128)S(1)}, f32[4,4,17,128]{3,1,2,0:T(4,128)}, u32[]{:S(2)}) %copy-start.3) | copy-done | bytes 139288
  3.2 0.1 reduce_sum.9
  3.3 0.0 copy-done.6
  3.4 0.1 copy-done.1
  3.5 0.2 multiply_subtract_fusion
  3.7 0.0 copy-start.2
  3.8 0.1 fusion.8
  3.9 0.9 %copy-done.2 = f32[4,17,17,128]{3,0,2,1:T(4,128)S(1)} copy-done((f32[4,17,17,128]{3,0,2,1:T(4,128)S(1)}, f32[4,17,17,128]{3,0,2,1:T(4,128)}, u32[]{:S(2)}) %copy-start.2) | copy-done | bytes 591896
  4.8 0.3 fusion
  5.1 0.0 copy-start
  5.1 0.1 reverse_select_fusion.diag_own
  5.2 0.6 %copy-done = s32[4,128]{1,0:T(4,128)S(1)} copy-done((s32[4,128]{1,0:T(4,128)S(1)}, s32[4,128]{1,0:T(4,128)}, u32[]{:S(2)}) %copy-start) | copy-done | bytes 2072
  5.8 40.0 %shard_map.91 = f32[4,17,128]{2,1,0:T(8,128)S(1)} custom-call(f32[4,17,17,128]{3,2,1,0:T(8,128)S(1)} %get-tuple-element.30.win_own, f32[4,17,17,128]{3,2,1,0:T(8,128)S(1)} %get-tuple-element.34.wout_own, f32[4,17,17,128]{3,2,1,0:T(8,128)S(1)} %reverse_select_fusion.diag_own, f32[17,17,128]{2,1,0:T(8,128)S(1)} %slice_bitcast_fusion.top_mat, ...), custom_call_target="tpu_custom_call" | custom-call | tf_op jit(solution)/shard_map/pallas_call | solution.py:336
  45.8 0.6 %copy.33 = f32[4,17,128]{2,0,1:T(4,128)} copy(f32[4,17,128]{2,1,0:T(8,128)S(1)} %reverse_select_fusion.4) | data formatting | bytes 69632 | tf_op jit(solution)/shard_map/jit(_where)/select_n | solution.py:328
  (14 shorter events, 0.2 us)
Async XLA Ops:
  0.0 1.5 %copy-start.4 = (f32[4,17,128]{2,0,1:T(4,128)S(1)}, f32[4,17,128]{2,0,1:T(4,128)}, u32[]{:S(2)}) copy-start(f32[4,17,128]{2,0,1:T(4,128)} %param.18) | copy-start | bytes 104452
  1.5 0.8 %copy-start.5 = (f32[4,17,128]{2,0,1:T(4,128)S(1)}, f32[4,17,128]{2,0,1:T(4,128)}, u32[]{:S(2)}) copy-start(f32[4,17,128]{2,0,1:T(4,128)} %param.19) | copy-start | bytes 104452
  2.3 0.9 %copy-start.3 = (f32[4,4,17,128]{3,1,2,0:T(4,128)S(1)}, f32[4,4,17,128]{3,1,2,0:T(4,128)}, u32[]{:S(2)}) copy-start(f32[4,4,17,128]{3,1,2,0:T(4,128)} %param.17) | copy-start | bytes 417796
  2.3 1.0 %copy-start.6 = (f32[4,17,128]{2,0,1:T(4,128)S(1)}, f32[4,17,128]{2,0,1:T(4,128)}, u32[]{:S(2)}) copy-start(f32[4,17,128]{2,0,1:T(4,128)} %param.16) | copy-start | bytes 104452
  2.3 1.2 %copy-start.1 = (f32[4,17,17,128]{3,0,2,1:T(4,128)S(1)}, f32[4,17,17,128]{3,0,2,1:T(4,128)}, u32[]{:S(2)}) copy-start(f32[4,17,17,128]{3,0,2,1:T(4,128)} %param.14) | copy-start | bytes 1775620
  3.7 1.1 %copy-start.2 = (f32[4,17,17,128]{3,0,2,1:T(4,128)S(1)}, f32[4,17,17,128]{3,0,2,1:T(4,128)}, u32[]{:S(2)}) copy-start(f32[4,17,17,128]{3,0,2,1:T(4,128)} %param.15) | copy-start | bytes 1775620
  5.1 0.7 %copy-start = (s32[4,128]{1,0:T(4,128)S(1)}, s32[4,128]{1,0:T(4,128)}, u32[]{:S(2)}) copy-start(s32[4,128]{1,0:T(4,128)} %neighbours.1) | copy-start | bytes 6148

commit v4 on v3

--- a/solution.py
+++ b/solution.py
@@ -258,7 +258,7 @@
             send_vec[...] = value
             return carry
 
-        lax.fori_loop(0, cells, forward, 0)
+        lax.fori_loop(0, cells, forward, 0, unroll=True)
 
         back = remote(vecs.at[0], x_in.at[sweep], x_send.at[sweep], x_recv.at[sweep], (outer, surf))
 
@@ -281,7 +281,7 @@
             vecs[t] = vecs[t] - matvec(coup.at[t], vecs.at[t + 1])
             return carry
 
-        lax.fori_loop(0, cells - 1, backward, 0)
+        lax.fori_loop(0, cells - 1, backward, 0, unroll=True)
 
         @pl.when(not_end)
         def _():

time: 46.7 us -> 46.7 us (level)
  no operation moved by 1% of the time
where the time goes in v4:
time: 46.7 us; the launch traced here: 46.3 us
  Pallas kernels  39.9 us (85%)
  local copies, waits for them, and re-layouts  4.82 us (10%)
  other arithmetic  1.44 us (3%)
    pallas_call x1, Pallas kernels, on_device(): pl.pallas_call(functools.partial(kernel, n_line, n_surf), out_shape=jax.S...  39.9 us
    unnamed x18, local copies, waits for them, and re-layouts  3.98 us

profile of v4, /device:TPU:0, one launch (start us, length us, event | category | flops | bytes accessed | tf_op | source)
XLA Modules:
  0.0 46.3 jit_solution(9583442368876253143)
XLA Ops:
  0.0 0.0 copy-start.4
  0.0 0.7 %copy.46 = f32[4,128]{1,0:T(4,128)S(1)} copy(f32[4,128]{1,0:T(4,128)} %param.13) | data formatting | bytes 4096
  0.7 0.1 scatter-add.6
  0.8 0.7 %fusion.7 = f32[1,128]{1,0:T(1,128)S(1)} fusion(s32[128]{0:T(128)} %param.21, f32[4,128]{1,0:T(4,128)S(1)} %scatter-add.6, f32[]{:T(128)S(6)} %convert_element_type.13), kind=kLoop, calls=%fused_computation.24 | loop fusion | flops 1280 | bytes 1540 | tf_op jit(solution)/shard_map/add | solution.py:316
  1.5 0.0 copy-done.4
  1.5 0.0 copy-start.5
  1.6 0.7 %copy-done.5 = f32[4,17,128]{2,0,1:T(4,128)S(1)} copy-done((f32[4,17,128]{2,0,1:T(4,128)S(1)}, f32[4,17,128]{2,0,1:T(4,128)}, u32[]{:S(2)}) %copy-start.5) | copy-done | bytes 34840
  2.3 0.0 copy-start.3
  2.3 0.0 copy-start.6
  2.3 0.0 copy-start.1
  2.3 0.9 %copy-done.3 = f32[4,4,17,128]{3,1,2,0:T(4,128)S(1)} copy-done((f32[4,4,17,128]{3,1,2,0:T(4,128)S(1)}, f32[4,4,17,128]{3,1,2,0:T(4,128)}, u32[]{:S(2)}) %copy-start.3) | copy-done | bytes 139288
  3.2 0.1 reduce_sum.9
  3.3 0.0 copy-done.6
  3.4 0.1 copy-done.1
  3.5 0.2 multiply_subtract_fusion
  3.7 0.0 copy-start.2
  3.8 0.1 fusion.8
  3.9 0.9 %copy-done.2 = f32[4,17,17,128]{3,0,2,1:T(4,128)S(1)} copy-done((f32[4,17,17,128]{3,0,2,1:T(4,128)S(1)}, f32[4,17,17,128]{3,0,2,1:T(4,128)}, u32[]{:S(2)}) %copy-start.2) | copy-done | bytes 591896
  4.8 0.3 fusion
  5.1 0.0 copy-start
  5.1 0.1 reverse_select_fusion.diag_own
  5.2 0.6 %copy-done = s32[4,128]{1,0:T(4,128)S(1)} copy-done((s32[4,128]{1,0:T(4,128)S(1)}, s32[4,128]{1,0:T(4,128)}, u32[]{:S(2)}) %copy-start) | copy-done | bytes 2072
  5.8 39.9 %shard_map.91 = f32[4,17,128]{2,1,0:T(8,128)S(1)} custom-call(f32[4,17,17,128]{3,2,1,0:T(8,128)S(1)} %get-tuple-element.30.win_own, f32[4,17,17,128]{3,2,1,0:T(8,128)S(1)} %get-tuple-element.34.wout_own, f32[4,17,17,128]{3,2,1,0:T(8,128)S(1)} %reverse_select_fusion.diag_own, f32[17,17,128]{2,1,0:T(8,128)S(1)} %slice_bitcast_fusion.top_mat, ...), custom_call_target="tpu_custom_call" | custom-call | tf_op jit(solution)/shard_map/pallas_call | solution.py:336
  45.7 0.6 %copy.33 = f32[4,17,128]{2,0,1:T(4,128)} copy(f32[4,17,128]{2,1,0:T(8,128)S(1)} %reverse_select_fusion.4) | data formatting | bytes 69632 | tf_op jit(solution)/shard_map/jit(_where)/select_n | solution.py:328
  (14 shorter events, 0.2 us)
Async XLA Ops:
  0.0 1.5 %copy-start.4 = (f32[4,17,128]{2,0,1:T(4,128)S(1)}, f32[4,17,128]{2,0,1:T(4,128)}, u32[]{:S(2)}) copy-start(f32[4,17,128]{2,0,1:T(4,128)} %param.18) | copy-start | bytes 104452
  1.5 0.8 %copy-start.5 = (f32[4,17,128]{2,0,1:T(4,128)S(1)}, f32[4,17,128]{2,0,1:T(4,128)}, u32[]{:S(2)}) copy-start(f32[4,17,128]{2,0,1:T(4,128)} %param.19) | copy-start | bytes 104452
  2.3 0.9 %copy-start.3 = (f32[4,4,17,128]{3,1,2,0:T(4,128)S(1)}, f32[4,4,17,128]{3,1,2,0:T(4,128)}, u32[]{:S(2)}) copy-start(f32[4,4,17,128]{3,1,2,0:T(4,128)} %param.17) | copy-start | bytes 417796
  2.3 1.0 %copy-start.6 = (f32[4,17,128]{2,0,1:T(4,128)S(1)}, f32[4,17,128]{2,0,1:T(4,128)}, u32[]{:S(2)}) copy-start(f32[4,17,128]{2,0,1:T(4,128)} %param.16) | copy-start | bytes 104452
  2.3 1.2 %copy-start.1 = (f32[4,17,17,128]{3,0,2,1:T(4,128)S(1)}, f32[4,17,17,128]{3,0,2,1:T(4,128)}, u32[]{:S(2)}) copy-start(f32[4,17,17,128]{3,0,2,1:T(4,128)} %param.14) | copy-start | bytes 1775620
  3.7 1.1 %copy-start.2 = (f32[4,17,17,128]{3,0,2,1:T(4,128)S(1)}, f32[4,17,17,128]{3,0,2,1:T(4,128)}, u32[]{:S(2)}) copy-start(f32[4,17,17,128]{3,0,2,1:T(4,128)} %param.15) | copy-start | bytes 1775620
  5.1 0.7 %copy-start = (s32[4,128]{1,0:T(4,128)S(1)}, s32[4,128]{1,0:T(4,128)}, u32[]{:S(2)}) copy-start(s32[4,128]{1,0:T(4,128)} %neighbours.1) | copy-start | bytes 6148

commit v5 on v3

--- a/solution.py
+++ b/solution.py
@@ -60,7 +60,7 @@
     n_line, n_surf,
     win_own, wout_own, diag_own, top_mat, top_coef, couple, rhs, start, neighbours,
     out,
-    win, wout, diag, edge_mat, edge_coef, edge_send, edge_recv,
+    win, wout, diag, step_mat, edge_mat, edge_coef, edge_send, edge_recv,
     dinv, coup, last, mid_inv, work, mat_in, vec_in, x_in, halo, prev, vecs, right, rprime, send_vec, onehot, stack, picked,
     mat_send, mat_recv, vec_send, vec_recv, x_send, x_recv, halo_send, halo_recv,
 ):
@@ -223,6 +223,15 @@
     @pl.when(is_mid)
     def _():
         mats_mid.start()
+
+    def chain(t, carry):
+        product(step_mat.at[t], win.at[t], dinv.at[t])
+        return carry
+
+    lax.fori_loop(0, cells, chain, 0)
+
+    @pl.when(is_mid)
+    def _():
         mats_mid.wait()
         product(mid_inv, mat_in.at[1], wout.at[cells - 1], work)
         invert_in_place(mid_inv)
@@ -241,6 +250,9 @@
         vec = remote(send_vec, vec_in.at[sweep, 0], vec_send.at[sweep, 0], vec_recv.at[sweep, 0], (inner, surf))
         vec_mid = remote(send_vec, vec_in.at[sweep, 1], vec_send.at[sweep, 1], vec_recv.at[sweep, 1], (inner, surf))
 
+        for t in range(cells):
+            vecs[t] = matvec(dinv.at[t], right.at[t])
+
         @pl.when(depth == 0)
         def _():
             vec_in[sweep, 0] = jnp.zeros((width, lines), jnp.float32)
@@ -249,16 +261,10 @@
         def _():
             vec.wait_recv()
 
-        send_vec[...] = vec_in[sweep, 0]
-
-        def forward(t, carry):
-            rprime[...] = right[t] - matvec(win.at[t], send_vec)
-            value = matvec(dinv.at[t], rprime)
-            vecs[t] = value
-            send_vec[...] = value
-            return carry
-
-        lax.fori_loop(0, cells, forward, 0)
+        for t in range(cells):
+            prior = vecs.at[t - 1] if t else vec_in.at[sweep, 0]
+            vecs[t] = vecs[t] - matvec(step_mat.at[t], prior)
+        send_vec[...] = vecs[cells - 1]
 
         back = remote(vecs.at[0], x_in.at[sweep], x_send.at[sweep], x_recv.at[sweep], (outer, surf))
 
@@ -272,6 +278,8 @@
         @pl.when(is_mid)
         def _():
             vec_mid.start()
+            prior = vecs.at[cells - 2] if cells > 1 else vec_in.at[sweep, 0]
+            rprime[...] = right[cells - 1] - matvec(win.at[cells - 1], prior)
             vec_mid.wait()
             rprime[...] = rprime[...] - matvec(wout.at[cells - 1], vec_in.at[sweep, 1])
             vecs[cells - 1] = matvec(mid_inv, rprime)
@@ -339,6 +347,7 @@
         in_specs=[vmem] * 9,
         out_specs=vmem,
         scratch_shapes=[
+            pltpu.VMEM((cells,) + mat, f32),
             pltpu.VMEM((cells,) + mat, f32),
             pltpu.VMEM((cells,) + mat, f32),
             pltpu.VMEM((cells,) + mat, f32),

time: 46.7 us -> 46.6 us (level)
  no operation moved by 1% of the time
where the time goes in v5:
time: 46.6 us; the launch traced here: 46.2 us
  Pallas kernels  39.8 us (85%)
  local copies, waits for them, and re-layouts  4.82 us (10%)
  other arithmetic  1.44 us (3%)
    pallas_call x1, Pallas kernels, on_device(): pl.pallas_call(functools.partial(kernel, n_line, n_surf), out_shape=jax.S...  39.8 us
    unnamed x18, local copies, waits for them, and re-layouts  3.98 us

profile of v5, /device:TPU:0, one launch (start us, length us, event | category | flops | bytes accessed | tf_op | source)
XLA Modules:
  0.0 46.2 jit_solution(10402381226481211326)
XLA Ops:
  0.0 0.0 copy-start.4
  0.0 0.7 %copy.46 = f32[4,128]{1,0:T(4,128)S(1)} copy(f32[4,128]{1,0:T(4,128)} %param.13) | data formatting | bytes 4096
  0.7 0.1 scatter-add.6
  0.8 0.7 %fusion.7 = f32[1,128]{1,0:T(1,128)S(1)} fusion(s32[128]{0:T(128)} %param.21, f32[4,128]{1,0:T(4,128)S(1)} %scatter-add.6, f32[]{:T(128)S(6)} %convert_element_type.13), kind=kLoop, calls=%fused_computation.24 | loop fusion | flops 1280 | bytes 1540 | tf_op jit(solution)/shard_map/add | solution.py:324
  1.5 0.0 copy-done.4
  1.5 0.0 copy-start.5
  1.6 0.7 %copy-done.5 = f32[4,17,128]{2,0,1:T(4,128)S(1)} copy-done((f32[4,17,128]{2,0,1:T(4,128)S(1)}, f32[4,17,128]{2,0,1:T(4,128)}, u32[]{:S(2)}) %copy-start.5) | copy-done | bytes 34840
  2.3 0.0 copy-start.3
  2.3 0.0 copy-start.6
  2.3 0.0 copy-start.1
  2.3 0.9 %copy-done.3 = f32[4,4,17,128]{3,1,2,0:T(4,128)S(1)} copy-done((f32[4,4,17,128]{3,1,2,0:T(4,128)S(1)}, f32[4,4,17,128]{3,1,2,0:T(4,128)}, u32[]{:S(2)}) %copy-start.3) | copy-done | bytes 139288
  3.2 0.1 reduce_sum.9
  3.3 0.0 copy-done.6
  3.4 0.1 copy-done.1
  3.5 0.2 multiply_subtract_fusion
  3.7 0.0 copy-start.2
  3.8 0.1 fusion.8
  3.9 0.9 %copy-done.2 = f32[4,17,17,128]{3,0,2,1:T(4,128)S(1)} copy-done((f32[4,17,17,128]{3,0,2,1:T(4,128)S(1)}, f32[4,17,17,128]{3,0,2,1:T(4,128)}, u32[]{:S(2)}) %copy-start.2) | copy-done | bytes 591896
  4.8 0.3 fusion
  5.1 0.0 copy-start
  5.1 0.1 reverse_select_fusion.diag_own
  5.2 0.6 %copy-done = s32[4,128]{1,0:T(4,128)S(1)} copy-done((s32[4,128]{1,0:T(4,128)S(1)}, s32[4,128]{1,0:T(4,128)}, u32[]{:S(2)}) %copy-start) | copy-done | bytes 2072
  5.8 39.8 %shard_map.91 = f32[4,17,128]{2,1,0:T(8,128)S(1)} custom-call(f32[4,17,17,128]{3,2,1,0:T(8,128)S(1)} %get-tuple-element.30.win_own, f32[4,17,17,128]{3,2,1,0:T(8,128)S(1)} %get-tuple-element.34.wout_own, f32[4,17,17,128]{3,2,1,0:T(8,128)S(1)} %reverse_select_fusion.diag_own, f32[17,17,128]{2,1,0:T(8,128)S(1)} %slice_bitcast_fusion.top_mat, ...), custom_call_target="tpu_custom_call" | custom-call | tf_op jit(solution)/shard_map/pallas_call | solution.py:344
  45.6 0.6 %copy.33 = f32[4,17,128]{2,0,1:T(4,128)} copy(f32[4,17,128]{2,1,0:T(8,128)S(1)} %reverse_select_fusion.4) | data formatting | bytes 69632 | tf_op jit(solution)/shard_map/jit(_where)/select_n | solution.py:336
  (14 shorter events, 0.2 us)
Async XLA Ops:
  0.0 1.5 %copy-start.4 = (f32[4,17,128]{2,0,1:T(4,128)S(1)}, f32[4,17,128]{2,0,1:T(4,128)}, u32[]{:S(2)}) copy-start(f32[4,17,128]{2,0,1:T(4,128)} %param.18) | copy-start | bytes 104452
  1.5 0.8 %copy-start.5 = (f32[4,17,128]{2,0,1:T(4,128)S(1)}, f32[4,17,128]{2,0,1:T(4,128)}, u32[]{:S(2)}) copy-start(f32[4,17,128]{2,0,1:T(4,128)} %param.19) | copy-start | bytes 104452
  2.3 0.9 %copy-start.3 = (f32[4,4,17,128]{3,1,2,0:T(4,128)S(1)}, f32[4,4,17,128]{3,1,2,0:T(4,128)}, u32[]{:S(2)}) copy-start(f32[4,4,17,128]{3,1,2,0:T(4,128)} %param.17) | copy-start | bytes 417796
  2.3 1.0 %copy-start.6 = (f32[4,17,128]{2,0,1:T(4,128)S(1)}, f32[4,17,128]{2,0,1:T(4,128)}, u32[]{:S(2)}) copy-start(f32[4,17,128]{2,0,1:T(4,128)} %param.16) | copy-start | bytes 104452
  2.3 1.2 %copy-start.1 = (f32[4,17,17,128]{3,0,2,1:T(4,128)S(1)}, f32[4,17,17,128]{3,0,2,1:T(4,128)}, u32[]{:S(2)}) copy-start(f32[4,17,17,128]{3,0,2,1:T(4,128)} %param.14) | copy-start | bytes 1775620
  3.7 1.1 %copy-start.2 = (f32[4,17,17,128]{3,0,2,1:T(4,128)S(1)}, f32[4,17,17,128]{3,0,2,1:T(4,128)}, u32[]{:S(2)}) copy-start(f32[4,17,17,128]{3,0,2,1:T(4,128)} %param.15) | copy-start | bytes 1775620
  5.1 0.7 %copy-start = (s32[4,128]{1,0:T(4,128)S(1)}, s32[4,128]{1,0:T(4,128)}, u32[]{:S(2)}) copy-start(s32[4,128]{1,0:T(4,128)} %neighbours.1) | copy-start | bytes 6148

commit v6 on v5

--- a/solution.py
+++ b/solution.py
@@ -61,7 +61,7 @@
     win_own, wout_own, diag_own, top_mat, top_coef, couple, rhs, start, neighbours,
     out,
     win, wout, diag, step_mat, edge_mat, edge_coef, edge_send, edge_recv,
-    dinv, coup, last, mid_inv, work, mat_in, vec_in, x_in, halo, prev, vecs, right, rprime, send_vec, onehot, stack, picked,
+    dinv, coup, last, mid_inv, work, mat_in, vec_in, x_in, halo, prev, vecs, right, rprime, send_vec, send_back, onehot, stack, picked,
     mat_send, mat_recv, vec_send, vec_recv, x_send, x_recv, halo_send, halo_recv,
 ):
     cells, width, _, lines = diag_own.shape
@@ -120,6 +120,8 @@
     ):
         hits = neighbours[slot : slot + 1, :] == source + base
         onehot[:, n * lines : (n + 1) * lines] = hits.astype(jnp.float32)
+    send_vec[...] = jnp.zeros_like(send_vec)
+    send_back[...] = jnp.zeros_like(send_back)
     for which in range(3):
         stack[which] = jnp.zeros_like(stack[which])
 
@@ -255,7 +257,7 @@
 
         @pl.when(depth == 0)
         def _():
-            vec_in[sweep, 0] = jnp.zeros((width, lines), jnp.float32)
+            vec_in[sweep, 0] = jnp.zeros(vec_in.shape[2:], jnp.float32)
 
         @pl.when(not_end)
         def _():
@@ -264,9 +266,9 @@
         for t in range(cells):
             prior = vecs.at[t - 1] if t else vec_in.at[sweep, 0]
             vecs[t] = vecs[t] - matvec(step_mat.at[t], prior)
-        send_vec[...] = vecs[cells - 1]
-
-        back = remote(vecs.at[0], x_in.at[sweep], x_send.at[sweep], x_recv.at[sweep], (outer, surf))
+        send_vec[0:width, :] = vecs[cells - 1]
+
+        back = remote(send_back, x_in.at[sweep], x_send.at[sweep], x_recv.at[sweep], (outer, surf))
 
         @pl.when(jnp.logical_not(is_mid))
         def _():
@@ -293,6 +295,7 @@
 
         @pl.when(not_end)
         def _():
+            send_back[0:width, :] = vecs[0]
             back.start()
             back.wait_send()
 
@@ -360,14 +363,15 @@
             pltpu.VMEM(mat, f32),
             pltpu.VMEM(mat, f32),
             pltpu.VMEM((2,) + mat, f32),
-            pltpu.VMEM((ITERS, 2) + vec, f32),
-            pltpu.VMEM((ITERS,) + vec, f32),
+            pltpu.VMEM((ITERS, 2, pad, lines), f32),
+            pltpu.VMEM((ITERS, pad, lines), f32),
             pltpu.VMEM((ITERS, 2, cells) + vec, f32),
             pltpu.VMEM((cells,) + vec, f32),
             pltpu.VMEM((cells,) + vec, f32),
             pltpu.VMEM((cells,) + vec, f32),
             pltpu.VMEM(vec, f32),
-            pltpu.VMEM(vec, f32),
+            pltpu.VMEM((pad, lines), f32),
+            pltpu.VMEM((pad, lines), f32),
             pltpu.VMEM((lines, 6 * lines), f32),
             pltpu.VMEM((3, 3 * cells * pad, lines), f32),
             pltpu.VMEM((3 * cells * pad, 6 * lines), f32),

time: 46.6 us -> 46.8 us (level)
  no operation moved by 1% of the time
where the time goes in v6:
time: 46.8 us; the launch traced here: 46.4 us
  Pallas kernels  40 us (85%)
  local copies, waits for them, and re-layouts  4.82 us (10%)
  other arithmetic  1.44 us (3%)
    pallas_call x1, Pallas kernels, on_device(): pl.pallas_call(functools.partial(kernel, n_line, n_surf), out_shape=jax.S...  40 us
    unnamed x18, local copies, waits for them, and re-layouts  3.98 us

profile of v6, /device:TPU:0, one launch (start us, length us, event | category | flops | bytes accessed | tf_op | source)
XLA Modules:
  0.0 46.4 jit_solution(3583559132568422694)
XLA Ops:
  0.0 0.0 copy-start.4
  0.0 0.7 %copy.46 = f32[4,128]{1,0:T(4,128)S(1)} copy(f32[4,128]{1,0:T(4,128)} %param.13) | data formatting | bytes 4096
  0.7 0.1 scatter-add.6
  0.8 0.7 %fusion.7 = f32[1,128]{1,0:T(1,128)S(1)} fusion(s32[128]{0:T(128)} %param.21, f32[4,128]{1,0:T(4,128)S(1)} %scatter-add.6, f32[]{:T(128)S(6)} %convert_element_type.13), kind=kLoop, calls=%fused_computation.24 | loop fusion | flops 1280 | bytes 1540 | tf_op jit(solution)/shard_map/add | solution.py:327
  1.5 0.0 copy-done.4
  1.5 0.0 copy-start.5
  1.6 0.7 %copy-done.5 = f32[4,17,128]{2,0,1:T(4,128)S(1)} copy-done((f32[4,17,128]{2,0,1:T(4,128)S(1)}, f32[4,17,128]{2,0,1:T(4,128)}, u32[]{:S(2)}) %copy-start.5) | copy-done | bytes 34840
  2.3 0.0 copy-start.3
  2.3 0.0 copy-start.6
  2.3 0.0 copy-start.1
  2.3 0.9 %copy-done.3 = f32[4,4,17,128]{3,1,2,0:T(4,128)S(1)} copy-done((f32[4,4,17,128]{3,1,2,0:T(4,128)S(1)}, f32[4,4,17,128]{3,1,2,0:T(4,128)}, u32[]{:S(2)}) %copy-start.3) | copy-done | bytes 139288
  3.2 0.1 reduce_sum.9
  3.3 0.0 copy-done.6
  3.4 0.1 copy-done.1
  3.5 0.2 multiply_subtract_fusion
  3.7 0.0 copy-start.2
  3.8 0.1 fusion.8
  3.9 0.9 %copy-done.2 = f32[4,17,17,128]{3,0,2,1:T(4,128)S(1)} copy-done((f32[4,17,17,128]{3,0,2,1:T(4,128)S(1)}, f32[4,17,17,128]{3,0,2,1:T(4,128)}, u32[]{:S(2)}) %copy-start.2) | copy-done | bytes 591896
  4.8 0.3 fusion
  5.1 0.0 copy-start
  5.1 0.1 reverse_select_fusion.diag_own
  5.2 0.6 %copy-done = s32[4,128]{1,0:T(4,128)S(1)} copy-done((s32[4,128]{1,0:T(4,128)S(1)}, s32[4,128]{1,0:T(4,128)}, u32[]{:S(2)}) %copy-start) | copy-done | bytes 2072
  5.8 40.0 %shard_map.91 = f32[4,17,128]{2,1,0:T(8,128)S(1)} custom-call(f32[4,17,17,128]{3,2,1,0:T(8,128)S(1)} %get-tuple-element.30.win_own, f32[4,17,17,128]{3,2,1,0:T(8,128)S(1)} %get-tuple-element.34.wout_own, f32[4,17,17,128]{3,2,1,0:T(8,128)S(1)} %reverse_select_fusion.diag_own, f32[17,17,128]{2,1,0:T(8,128)S(1)} %slice_bitcast_fusion.top_mat, ...), custom_call_target="tpu_custom_call" | custom-call | tf_op jit(solution)/shard_map/pallas_call | solution.py:347
  45.8 0.6 %copy.33 = f32[4,17,128]{2,0,1:T(4,128)} copy(f32[4,17,128]{2,1,0:T(8,128)S(1)} %reverse_select_fusion.4) | data formatting | bytes 69632 | tf_op jit(solution)/shard_map/jit(_where)/select_n | solution.py:339
  (14 shorter events, 0.2 us)
Async XLA Ops:
  0.0 1.5 %copy-start.4 = (f32[4,17,128]{2,0,1:T(4,128)S(1)}, f32[4,17,128]{2,0,1:T(4,128)}, u32[]{:S(2)}) copy-start(f32[4,17,128]{2,0,1:T(4,128)} %param.18) | copy-start | bytes 104452
  1.5 0.8 %copy-start.5 = (f32[4,17,128]{2,0,1:T(4,128)S(1)}, f32[4,17,128]{2,0,1:T(4,128)}, u32[]{:S(2)}) copy-start(f32[4,17,128]{2,0,1:T(4,128)} %param.19) | copy-start | bytes 104452
  2.3 0.9 %copy-start.3 = (f32[4,4,17,128]{3,1,2,0:T(4,128)S(1)}, f32[4,4,17,128]{3,1,2,0:T(4,128)}, u32[]{:S(2)}) copy-start(f32[4,4,17,128]{3,1,2,0:T(4,128)} %param.17) | copy-start | bytes 417796
  2.3 1.0 %copy-start.6 = (f32[4,17,128]{2,0,1:T(4,128)S(1)}, f32[4,17,128]{2,0,1:T(4,128)}, u32[]{:S(2)}) copy-start(f32[4,17,128]{2,0,1:T(4,128)} %param.16) | copy-start | bytes 104452
  2.3 1.2 %copy-start.1 = (f32[4,17,17,128]{3,0,2,1:T(4,128)S(1)}, f32[4,17,17,128]{3,0,2,1:T(4,128)}, u32[]{:S(2)}) copy-start(f32[4,17,17,128]{3,0,2,1:T(4,128)} %param.14) | copy-start | bytes 1775620
  3.7 1.1 %copy-start.2 = (f32[4,17,17,128]{3,0,2,1:T(4,128)S(1)}, f32[4,17,17,128]{3,0,2,1:T(4,128)}, u32[]{:S(2)}) copy-start(f32[4,17,17,128]{3,0,2,1:T(4,128)} %param.15) | copy-start | bytes 1775620
  5.1 0.7 %copy-start = (s32[4,128]{1,0:T(4,128)S(1)}, s32[4,128]{1,0:T(4,128)}, u32[]{:S(2)}) copy-start(s32[4,128]{1,0:T(4,128)} %neighbours.1) | copy-start | bytes 6148
